TPU v7x, 128 devices: a whole 4x4x4 slice. The times are simulated.
128 devices in a mesh: frm: 8 (over y_lo, z), pat: 16 (over x, y_hi, core).
Axes of the slice: x: 4, y: 4 (y_hi: 2, y_lo: 2; y = y_hi * 2 + y_lo), z: 4, core: 2. Of those that a mesh axis runs over, the one named last changes fastest.
Arguments:
- frames: float32 [8, 2048, 2048], P('frm', 'pat'), may hold values from -6 to 6
- shifts: float32 [8, 2], P('frm'), may hold values from -0.5 to 0.5
- coefficients: float32 [8, 512, 40], P('frm', 'pat'), may hold values from -0.9 to 0.9
- anchors: int32 [512, 2], P('pat'), may hold values from 0 to 1960, as said below
- assign: int32 [512], P('pat'), may hold values from 0 to 15, as said below
Outputs:
- new_coefficients: float32 [8, 512, 40], P('frm', 'pat')
- object_spectra: float32 [512, 2, 7744], P(('pat', 'frm'))
Inputs may be any that keep to these rules, and one draw needn't show every extreme that they name: `anchors`: the anchor row of patch p lies in p // 32 * 128 to p // 32 * 128 + 127 and is at most 1960; the anchor column is at most 1960. `assign`: among the 32 patches p of one value of p // 32, exactly 2 carry each group number.
All inputs are finite; a program needn't handle non-finite values.
Results may differ from a plain program's by a relative error of at most 0.0003.
Values sent between devices are 32-bit elements; how exact they have to be, the bound alone decides.
A program may use at most 128 MiB of HBM per device.

v0:
```python
import math

import jax
import jax.numpy as jnp
from jax import lax
from jax.sharding import PartitionSpec as P

PATCH = 88
MODES = 40
ITERS = 2
FPD = 1
SH = 128
PPS = 32


damping = 0.05
step_size = 64.0
highest = lax.Precision.HIGHEST


def shifted(value, axis, steps):
    count = lax.axis_size(axis)
    first, last = (max(0, -steps), min(count, count - steps))
    return lax.ppermute(value, axis, [(source, source + steps) for source in range(first, last)])


def sent_together(arrays, axis, split_dim, concat_dim, along):
    widths = [a.shape[along] for a in arrays]
    both = jnp.concatenate(arrays, axis=along)
    filled = lax.all_to_all(both, axis, split_axis=split_dim, concat_axis=concat_dim, tiled=True)
    return tuple(jnp.split(filled, [sum(widths[:k]) for k in range(1, len(widths))], axis=along))


def noll_index(j):
    n = 0
    remaining = j - 1
    while remaining > n:
        n += 1
        remaining -= n
    m = (-1) ** j * (n % 2 + 2 * ((remaining + (n + 1) % 2) // 2))
    return (n, m)


def zernike_table(length, number):
    centre = length / 2.0
    coords = (jnp.arange(length, dtype=jnp.float32) - centre) / (length / 4.0)
    row_grid = jnp.broadcast_to(coords[:, None], (length, length))
    col_grid = jnp.broadcast_to(coords[None, :], (length, length))
    radius = jnp.sqrt(row_grid * row_grid + col_grid * col_grid)
    angle_grid = jnp.arctan2(row_grid, col_grid)
    inside = (radius <= 1.0).astype(jnp.float32)
    surfaces = []
    for j in range(2, number + 2):
        n, m = noll_index(j)
        order_abs = abs(m)
        radial = jnp.zeros((length, length), jnp.float32)
        for k in range((n - order_abs) // 2 + 1):
            factor = (
                (-1) ** k
                * math.factorial(n - k)
                / (
                    math.factorial(k)
                    * math.factorial((n + order_abs) // 2 - k)
                    * math.factorial((n - order_abs) // 2 - k)
                )
            )
            radial = radial + factor * radius ** (n - 2 * k)
        if m == 0:
            surface = math.sqrt(n + 1) * radial
        elif m > 0:
            surface = math.sqrt(2 * (n + 1)) * radial * jnp.cos(order_abs * angle_grid)
        else:
            surface = math.sqrt(2 * (n + 1)) * radial * jnp.sin(order_abs * angle_grid)
        surfaces.append(surface * inside)
    return (jnp.stack(surfaces), inside)


def window_table(length):
    ramp_index = jnp.arange(length, dtype=jnp.float32)
    profile = 0.5 - 0.5 * jnp.cos(2.0 * jnp.pi * (ramp_index + 0.5) / length)
    return profile[:, None] * profile[None, :]


def signed_frequencies(length):
    ramp_index = jnp.arange(length, dtype=jnp.int32)
    return ((ramp_index + length // 2) % length - length // 2).astype(jnp.float32)


def apply_rows(table, values):
    return jnp.einsum("uk,kvb->uvb", table, values, precision=highest)


def apply_columns(table, values):
    return jnp.einsum("vk,ukb->uvb", table, values, precision=highest)


def complex_pass(applier, table_real, table_imag, real_in, imag_in):
    if imag_in is None:
        return (applier(table_real, real_in), applier(table_imag, real_in))
    real_out = applier(table_real, real_in) - applier(table_imag, imag_in)
    imag_out = applier(table_real, imag_in) + applier(table_imag, real_in)
    return (real_out, imag_out)


def fourier_pair(real_in, imag_in, table_real, table_imag):
    first_real, first_imag = complex_pass(apply_rows, table_real, table_imag, real_in, imag_in)
    return complex_pass(apply_columns, table_real, table_imag, first_real, first_imag)


def shards(frames, shifts, coefficients, anchors, assign):
    mode_table, aperture = zernike_table(PATCH, MODES)
    zernike_flat = mode_table.reshape(MODES, PATCH * PATCH)
    spread_scale = 1.0 / (PATCH * PATCH * jnp.sum(aperture))
    window = window_table(PATCH)
    index_grid = jnp.arange(PATCH, dtype=jnp.int32)
    product_grid = index_grid[:, None] * index_grid[None, :] % PATCH
    angles = 2.0 * jnp.pi * product_grid.astype(jnp.float32) / PATCH
    cosine_table = jnp.cos(angles)
    sine_table = jnp.sin(angles)
    frame_groups = lax.axis_size("frm")
    total_frames = FPD * frame_groups
    lower_rows = shifted(frames[:, : PATCH - 1, :], "pat", -1)
    extended = jnp.concatenate([frames, lower_rows], axis=1)
    first_row = lax.axis_index("pat") * SH

    def cut_patch(anchor):
        return lax.dynamic_slice(
            extended, (anchor[0] * 0, anchor[0] - first_row, anchor[1]), (FPD, PATCH, PATCH)
        )

    patch_data = jax.vmap(cut_patch)(anchors)
    ordering = jnp.argsort(assign * PPS + jnp.arange(PPS, dtype=jnp.int32))
    patch_data = jnp.transpose(patch_data[ordering], (1, 0, 2, 3)).reshape(FPD, PPS, PATCH * PATCH)
    local_coefs = coefficients[:, ordering]
    shift_rows = jnp.broadcast_to(shifts[:, None, :], (FPD, PPS, 2))
    patch_data, local_coefs, shift_rows = sent_together(
        (patch_data, local_coefs, shift_rows), "pat", 1, 1, 2
    )
    patch_data, local_coefs, shift_rows = (
        lax.all_to_all(patch_data, "frm", split_axis=1, concat_axis=0, tiled=True),
        lax.all_to_all(local_coefs, "frm", split_axis=1, concat_axis=0, tiled=True),
        lax.all_to_all(shift_rows, "frm", split_axis=1, concat_axis=0, tiled=True),
    )
    frames_here = local_coefs.shape[0]
    patches_here = local_coefs.shape[1]
    item_count = frames_here * patches_here
    spatial = (
        jnp.transpose(patch_data.reshape(item_count, PATCH * PATCH)).reshape(
            PATCH, PATCH, item_count
        )
        * window[:, :, None]
    )
    spectrum_real, spectrum_imag = fourier_pair(spatial, None, cosine_table, -sine_table)
    frequencies = signed_frequencies(PATCH)
    item_shifts = shift_rows.reshape(item_count, 2)
    ramp_angle = (
        -2.0
        * jnp.pi
        / PATCH
        * (
            frequencies[:, None, None] * item_shifts[None, None, :, 0]
            + frequencies[None, :, None] * item_shifts[None, None, :, 1]
        )
    )
    ramp_cos = jnp.cos(ramp_angle)
    ramp_sin = jnp.sin(ramp_angle)
    data_real = spectrum_real * ramp_cos - spectrum_imag * ramp_sin
    data_imag = spectrum_real * ramp_sin + spectrum_imag * ramp_cos

    def frame_total(values):
        return jnp.sum(values.reshape(PATCH, PATCH, frames_here, patches_here), axis=2)

    def spread_frames(values):
        return jnp.broadcast_to(
            values[:, :, None, :], (PATCH, PATCH, frames_here, patches_here)
        ).reshape(PATCH, PATCH, item_count)

    energy_local = jnp.sum(frame_total(data_real**2 + data_imag**2), axis=(0, 1))
    current = local_coefs.reshape(item_count, MODES)
    share_real = data_real[:, :, :1]
    share_imag = data_imag[:, :, :1]
    for iteration in range(ITERS):
        phases = jnp.dot(
            jnp.transpose(zernike_flat), jnp.transpose(current), precision=highest
        ).reshape(PATCH, PATCH, item_count)
        pupil_real = aperture[:, :, None] * jnp.cos(phases)
        pupil_imag = aperture[:, :, None] * jnp.sin(phases)
        focal_real, focal_imag = fourier_pair(pupil_real, pupil_imag, cosine_table, -sine_table)
        spread = spread_scale * (focal_real**2 + focal_imag**2)
        transfer_real, transfer_imag = fourier_pair(spread, None, cosine_table, -sine_table)
        cross_real = frame_total(data_real * transfer_real + data_imag * transfer_imag)
        cross_imag = frame_total(data_imag * transfer_real - data_real * transfer_imag)
        transfer_power = frame_total(transfer_real**2 + transfer_imag**2)
        denominator = transfer_power + damping
        estimate_real = cross_real / denominator
        estimate_imag = cross_imag / denominator
        share_real = estimate_real
        share_imag = estimate_imag
        full_real = spread_frames(estimate_real)
        full_imag = spread_frames(estimate_imag)
        misfit_real = data_real - (full_real * transfer_real - full_imag * transfer_imag)
        misfit_imag = data_imag - (full_real * transfer_imag + full_imag * transfer_real)
        grad_real = -2.0 * (full_real * misfit_real + full_imag * misfit_imag)
        grad_imag = -2.0 * (full_real * misfit_imag - full_imag * misfit_real)
        grad_spread, unused = fourier_pair(grad_real, grad_imag, cosine_table, sine_table)
        weight = 2.0 * spread_scale * grad_spread
        back_real, back_imag = fourier_pair(
            weight * focal_real, weight * focal_imag, cosine_table, sine_table
        )
        grad_phase = back_imag * pupil_real - back_real * pupil_imag
        grad_coef = jnp.dot(
            zernike_flat, grad_phase.reshape(PATCH * PATCH, item_count), precision=highest
        )
        item_energy = jnp.broadcast_to(energy_local[None, :], (frames_here, patches_here)).reshape(
            item_count
        )
        current = (
            current - step_size * total_frames * jnp.transpose(grad_coef) / item_energy[:, None]
        )
    finals = current.reshape(frames_here, patches_here, MODES)
    finals = lax.all_to_all(finals, "frm", split_axis=0, concat_axis=1, tiled=True)
    finals = lax.all_to_all(finals, "pat", split_axis=1, concat_axis=1, tiled=True)
    new_coefficients = jnp.zeros_like(finals).at[:, ordering].set(finals)
    stacked = jnp.stack([share_real, share_imag], axis=0).reshape(
        2, PATCH * PATCH, share_real.shape[2]
    )
    object_spectra = jnp.transpose(stacked, (2, 0, 1)) / PATCH
    return (new_coefficients, object_spectra)


def solution(mesh):
    in_specs = (
        P("frm", "pat", None),
        P("frm", None),
        P("frm", "pat", None),
        P("pat", None),
        P("pat"),
    )
    out_specs = (P("frm", "pat", None), P(("pat", "frm"), None, None))
    return jax.shard_map(shards, mesh=mesh, in_specs=in_specs, out_specs=out_specs, check_vma=False)
```

profile of v0, /device:TPU:7, one launch (start us, length us, event | category | flops | bytes accessed | tf_op | source)
XLA Modules:
  0.0 373.7 jit_solution(14936336515914465043)
XLA Ops:
  2.5 2.6 collective-permute-start
  8.0 2.9 multiply_select_fusion.42
  10.9 8.6 %multiply_select_fusion.64 = (f32[1,7744]{1,0:T(1,128)}, f32[1,7744]{1,0:T(1,128)S(1)}, f32[1,7744]{1,0:T(1,128)}, f32[1,7744]{1,0:T(1,128)}, f32[1,7744]{1,0:T(...) fusion(f32[1,7744]{1,0:T(1,128)S(1)} %get-tuple-element.120, ...), kind=kLoop, calls=%fused_computation.359 | loop fusion | flops 1122880 | bytes 1270016 | tf_op jit(solution)/shard_map/mul | solution.py:74
  23.6 85.3 %while.1 = (s32[]{:T(128)}, f32[1,215,2048]{2,1,0:T(8,128)S(1)}, s32[32,3]{0,1:T(4,128)S(1)}, f32[32,1,88,88]{3,2,1,0:T(8,128)}, s32[]{:T(128)}) while((s32[]{:T(128)}, f32[1,215,2048]{2,1,0:T(8,128)S(1)}, s32[32,3]{0,1:T(4,128)S(1)}, f32[32,1,88,88]{3,2,1,0:T(8,128)}, s32[]{:T(128)}) %tuple.153), condition=%wide.while_cond, body=%wide.while_body.sunk | while | flops 2 | bytes 77673 | solution.py:127
  113.2 3.9 %concatenate.13 = f32[1,32,7786]{2,0,1:T(1,128)} concatenate(f32[1,32,7744]{2,0,1:T(1,128)S(1)} %reshape_transpose.3, f32[1,32,40]{2,0,1:T(1,128)S(1)} %bitcast.460, f32[1,32,2]{2,0,1:T(1,128)S(1)} %broadcast_in_dim.1010), dimensions={2} | concatenate | bytes 1993216 | tf_op jit(solution)/shard_map/concatenate | solution.py:29
  117.5 7.3 %all-to-all-start = ((f32[1,32,7786]{2,0,1:T(1,128)}), f32[1,32,7786]{2,0,1:T(1,128)}, u32[]{:S(2)}, u32[]{:S(2)}) async-start(f32[1,32,7786]{2,0,1:T(1,128)} %concatenate.13), calls=%async_computation | async-start | bytes 1998848 | tf_op jit(solution)/shard_map/all_to_all | solution.py:30
  124.8 14.3 %multiply_select_fusion = (f32[1,88,88]{2,0,1:T(1,128)S(1)}, f32[1,88,88]{2,0,1:T(1,128)S(1)}, f32[1,88,88]{2,0,1:T(1,128)S(1)}, f32[1,88,88]{2,0,1:T(1,128)S(1)...) fusion(f32[88]{0:T(128)S(1)} %get-tuple-element.171, ...), kind=kLoop, calls=%fused_computation.266 | loop fusion | flops 1409408 | bytes 1239744 | tf_op jit(solution)/shard_map/mul | solution.py:74
  143.9 10.1 %stack.7 = f32[40,88,88]{2,0,1:T(8,128)} concatenate(f32[1,88,88]{2,0,1:T(1,128)} %get-tuple-element.158, f32[1,88,88]{2,0,1:T(1,128)} %get-tuple-element.151, f32[1,88,88]{2,0,1:T(1,128)} %get-tuple-element.168, f32[1,88,88]{2,0,1:T(1,128)} %get-tuple-element.150, f32[1,88,88]{2,0,1:T(1,128)} %get-tuple-element.152, f32[1,88,88]{2,0,1:T(1,128)S(1)} %get-tuple-element.126, ...), dimensions={0} | concatenate | bytes 2478080 | tf_op jit(solution)/shard_map/stack | solution.py:75
  155.7 5.7 %all-to-all-start.3 = ((f32[1,32,2]{2,0,1:T(1,128)}), f32[1,32,2]{2,0,1:T(1,128)S(1)}, u32[]{:S(2)}, u32[]{:S(2)}) async-start(f32[1,32,2]{2,0,1:T(1,128)} %split.14), calls=%async_computation.3 | async-start | bytes 32768 | tf_op jit(solution)/shard_map/all_to_all | solution.py:142
  164.2 2.3 all-to-all-done.3
  166.5 3.3 all-to-all-start.1
  170.6 4.2 %all-to-all-done.1 = f32[8,1,160]{2,1,0:T(1,128)S(1)} async-done(((f32[8,1,160]{2,1,0:T(1,128)}), f32[8,1,160]{2,1,0:T(1,128)S(1)}, u32[]{:S(2)}, u32[]{:S(2)}) %all-to-all-start.1) | async-done | bytes 5152 | tf_op jit(solution)/shard_map/all_to_all | solution.py:141
  174.8 3.6 all-to-all-start.2
  179.1 7.9 %cosine_multiply_fusion.1 = (f32[88,88,32]{1,2,0:T(8,128)S(1)}, f32[88,88,32]{1,2,0:T(8,128)S(1)}) fusion(f32[88,88]{1,0:T(8,128)S(1)} %fusion.250, f32[32,40,1]{1,0,2:T(8,128)S(1)} %bitcast.458, f32[88,88,40]{1,0,2:T(8,128)S(1)} %dot_general.209), kind=kOutput, calls=%fused_computation.123 | convolution fusion | flops 119443456 | bytes 3257600 | tf_op jit(solution)/shard_map/dot_general | solution.py:183
  205.3 2.6 fusion.183
  209.4 2.6 fusion.7
  220.8 7.5 %add_reduce_fusion = (f32[32]{0:T(128)S(1)}, f32[88,88,32]{1,0,2:T(8,128)S(1)}, f32[88,88,32]{1,0,2:T(8,128)S(1)}) fusion(f32[88,88,32]{1,0,2:T(8,128)S(1)} %fusion.9, f32[88,32]{0,1:T(8,128)S(1)} %copy-done.65, f32[88,32]{0,1:T(8,128)S(1)} %copy-done.64, f32[88,32,88]{2,0,1:T(8,128)S(1)} %fusion.194, f32[88,88,32]{1,0,2:T(8,128)S(1)} %fusion.74), kind=kOutput, calls=%fused_computation.116 | convolution fusion | flops 264984160 | bytes 4978816 | tf_op jit(solution)/shard_map/vk,ukb->uvb/dot_general | solution.py:94
  228.3 4.4 %multiply_add_fusion.3 = (f32[88,88,32]{1,0,2:T(8,128)}, f32[88,88,32]{1,0,2:T(8,128)}, f32[88,88,32]{1,0,2:T(8,128)}, f32[88,88,32]{1,0,2:T(8,128)}) fusion(f32[88,88,32]{1,0,2:T(8,128)S(1)} %get-tuple-element.21, f32[88,88,32]{1,0,2:T(8,128)S(1)} %get-tuple-element.22, f32[88,88,32]{1,0,2:T(8,128)S(1)} %copy-done.19, f32[88,32,88]{2,0,1:T(8,128)S(1)} %copy-done.23, ...), kind=kOutput, calls=%fused_computation.119 | convolution fusion | flops 264240768 | bytes 8921088 | tf_op jit(solution)/shard_map/vk,ukb->uvb/dot_general | solution.py:94
  237.2 2.6 fusion.19
  252.3 2.6 fusion.124
  254.9 2.6 fusion.171
  260.8 2.7 fusion.122
  263.4 2.6 fusion.174
  266.2 6.7 %fusion.97 = f32[32,40]{1,0:T(8,128)S(1)} fusion(f32[32,40]{1,0:T(8,128)S(1)} %bitcast.459, f32[40,88,88]{2,0,1:T(8,128)} %stack.7, f32[88,88,32]{1,2,0:T(8,128)} %copy-done.11, f32[88,88,32]{1,2,0:T(8,128)} %copy-done.10, f32[88,32,88]{2,0,1:T(8,128)} %fusion.122, f32[88,32,88]{2,0,1:T(8,128)} %fusion.171, f32[88,32,88]{2,0,1:T(8,128)} %fusion.124, ...), kind=kOutput, calls=%fused_computation.151 | convolution fusion | flops 120190720 | bytes 7196800 | tf_op jit(solution)/shard_map/dot_general | solution.py:211
  272.9 7.7 %cosine_multiply_fusion = (f32[88,88,32]{1,2,0:T(8,128)S(1)}, f32[88,88,32]{1,2,0:T(8,128)S(1)}) fusion(f32[88,88]{1,0:T(8,128)S(1)} %fusion.250, f32[32,40]{1,0:T(8,128)S(1)} %fusion.97, f32[88,88,40]{1,0,2:T(8,128)S(1)} %copy-done.17), kind=kOutput, calls=%fused_computation.115 | convolution fusion | flops 119443456 | bytes 3257600 | tf_op jit(solution)/shard_map/dot_general | solution.py:183
  303.6 4.6 %multiply_add_fusion.1 = (f32[88,88,32]{1,0,2:T(8,128)}, f32[88,88,32]{1,0,2:T(8,128)}, f32[88,88,32]{1,0,2:T(8,128)}, f32[88,88,32]{1,0,2:T(8,128)}) fusion(f32[88,88,32]{1,0,2:T(8,128)S(1)} %get-tuple-element.21, f32[88,88,32]{1,0,2:T(8,128)S(1)} %get-tuple-element.22, f32[88,88,32]{1,0,2:T(8,128)S(1)} %fusion.5, f32[88,32,88]{2,0,1:T(8,128)S(1)} %fusion.160, ...), kind=kOutput, calls=%fused_computation.112 | convolution fusion | flops 264240768 | bytes 8921088 | tf_op jit(solution)/shard_map/vk,ukb->uvb/dot_general | solution.py:94
  315.0 2.6 fusion.27
  339.4 2.9 fusion.88
  343.0 5.1 %all-to-all-start.4 = ((f32[8,1,160]{2,1,0:T(1,128)}), f32[8,1,160]{2,1,0:T(1,128)S(1)}, u32[]{:S(2)}, u32[]{:S(2)}) async-start(f32[8,1,160]{2,1,0:T(1,128)} %reshape.5391), calls=%async_computation.4 | async-start | bytes 16384 | tf_op jit(solution)/shard_map/all_to_all | solution.py:221
  348.5 4.5 %all-to-all-done.4 = f32[8,1,160]{2,1,0:T(1,128)S(1)} async-done(((f32[8,1,160]{2,1,0:T(1,128)}), f32[8,1,160]{2,1,0:T(1,128)S(1)}, u32[]{:S(2)}, u32[]{:S(2)}) %all-to-all-start.4) | async-done | bytes 5152 | tf_op jit(solution)/shard_map/all_to_all | solution.py:221
  354.4 12.1 %all-to-all-start.5 = ((f32[1,32,40]{2,0,1:T(1,128)}), f32[1,32,40]{2,0,1:T(1,128)S(1)}, u32[]{:S(2)}, u32[]{:S(2)}) async-start(f32[1,32,40]{2,0,1:T(1,128)} %bitcast.45), calls=%async_computation.5 | async-start | bytes 32768 | tf_op jit(solution)/shard_map/all_to_all | solution.py:222
  367.5 4.6 %all-to-all-done.5 = f32[1,32,40]{2,0,1:T(1,128)S(1)} async-done(((f32[1,32,40]{2,0,1:T(1,128)}), f32[1,32,40]{2,0,1:T(1,128)S(1)}, u32[]{:S(2)}, u32[]{:S(2)}) %all-to-all-start.5) | async-done | bytes 5152 | tf_op jit(solution)/shard_map/all_to_all | solution.py:222
  (360 shorter events, 212.3 us)
Async XLA Ops:
  2.5 20.7 %collective-permute-start = (f32[1,87,2048]{2,0,1:T(1,128)S(1)}, f32[1,87,2048]{2,0,1:T(1,128)S(1)}, u32[]{:S(2)}, u32[]{:S(2)}) collective-permute-start(f32[1,87,2048]{2,0,1:T(1,128)S(1)} %copy.27), channel_id=1, source_target_pairs={{1,0},{2,1},{3,2},{4,3},{5,4},{6,5},{7,6},{8,7},{9,8},{10,9},{11,1... | collective-permute-start | bytes 2138120 | tf_op jit(solution)/shard_map/ppermute | solution.py:24
  117.2 22.1 %copy-start.29 = (f32[1,7744]{1,0:T(1,128)S(1)}, f32[1,7744]{1,0:T(1,128)}, u32[]{:S(2)}) copy-start(f32[1,7744]{1,0:T(1,128)} %get-tuple-element.33) | copy-start | bytes 92932
  117.2 22.1 %copy-start.30 = (f32[1,7744]{1,0:T(1,128)S(1)}, f32[1,7744]{1,0:T(1,128)}, u32[]{:S(2)}) copy-start(f32[1,7744]{1,0:T(1,128)} %get-tuple-element.81) | copy-start | bytes 92932
  117.2 22.1 %copy-start.31 = (f32[1,7744]{1,0:T(1,128)S(1)}, f32[1,7744]{1,0:T(1,128)}, u32[]{:S(2)}) copy-start(f32[1,7744]{1,0:T(1,128)} %get-tuple-element.84) | copy-start | bytes 92932
  117.2 22.1 %copy-start.32 = (f32[1,7744]{1,0:T(1,128)S(1)}, f32[1,7744]{1,0:T(1,128)}, u32[]{:S(2)}) copy-start(f32[1,7744]{1,0:T(1,128)} %get-tuple-element.85) | copy-start | bytes 92932
  117.2 22.1 %copy-start.33 = (f32[1,7744]{1,0:T(1,128)S(1)}, f32[1,7744]{1,0:T(1,128)}, u32[]{:S(2)}) copy-start(f32[1,7744]{1,0:T(1,128)} %get-tuple-element.86) | copy-start | bytes 92932
  117.2 22.1 %copy-start.34 = (f32[1,7744]{1,0:T(1,128)S(1)}, f32[1,7744]{1,0:T(1,128)}, u32[]{:S(2)}) copy-start(f32[1,7744]{1,0:T(1,128)} %get-tuple-element.87) | copy-start | bytes 92932
  117.2 22.1 %copy-start.35 = (f32[1,7744]{1,0:T(1,128)S(1)}, f32[1,7744]{1,0:T(1,128)}, u32[]{:S(2)}) copy-start(f32[1,7744]{1,0:T(1,128)} %get-tuple-element.88) | copy-start | bytes 92932
  117.2 22.1 %copy-start.36 = (f32[1,7744]{1,0:T(1,128)S(1)}, f32[1,7744]{1,0:T(1,128)}, u32[]{:S(2)}) copy-start(f32[1,7744]{1,0:T(1,128)} %get-tuple-element.89) | copy-start | bytes 92932
  117.2 22.1 %copy-start.37 = (f32[1,7744]{1,0:T(1,128)S(1)}, f32[1,7744]{1,0:T(1,128)}, u32[]{:S(2)}) copy-start(f32[1,7744]{1,0:T(1,128)} %get-tuple-element.90) | copy-start | bytes 92932
  117.3 22.1 %copy-start.38 = (f32[1,7744]{1,0:T(1,128)S(1)}, f32[1,7744]{1,0:T(1,128)}, u32[]{:S(2)}) copy-start(f32[1,7744]{1,0:T(1,128)} %get-tuple-element.91) | copy-start | bytes 92932
  117.3 22.1 %copy-start.39 = (f32[1,7744]{1,0:T(1,128)S(1)}, f32[1,7744]{1,0:T(1,128)}, u32[]{:S(2)}) copy-start(f32[1,7744]{1,0:T(1,128)} %get-tuple-element.92) | copy-start | bytes 92932
  117.3 22.1 %copy-start.40 = (f32[1,7744]{1,0:T(1,128)S(1)}, f32[1,7744]{1,0:T(1,128)}, u32[]{:S(2)}) copy-start(f32[1,7744]{1,0:T(1,128)} %get-tuple-element.93) | copy-start | bytes 92932
  117.3 22.1 %copy-start.41 = (f32[1,7744]{1,0:T(1,128)S(1)}, f32[1,7744]{1,0:T(1,128)}, u32[]{:S(2)}) copy-start(f32[1,7744]{1,0:T(1,128)} %get-tuple-element.94) | copy-start | bytes 92932
  117.3 22.1 %copy-start.42 = (f32[1,7744]{1,0:T(1,128)S(1)}, f32[1,7744]{1,0:T(1,128)}, u32[]{:S(2)}) copy-start(f32[1,7744]{1,0:T(1,128)} %get-tuple-element.95) | copy-start | bytes 92932
  117.3 22.1 %copy-start.43 = (f32[1,7744]{1,0:T(1,128)S(1)}, f32[1,7744]{1,0:T(1,128)}, u32[]{:S(2)}) copy-start(f32[1,7744]{1,0:T(1,128)} %get-tuple-element.96) | copy-start | bytes 92932
  117.3 22.1 %copy-start.44 = (f32[1,7744]{1,0:T(1,128)S(1)}, f32[1,7744]{1,0:T(1,128)}, u32[]{:S(2)}) copy-start(f32[1,7744]{1,0:T(1,128)} %get-tuple-element.97) | copy-start | bytes 92932
  117.3 22.1 %copy-start.45 = (f32[1,7744]{1,0:T(1,128)S(1)}, f32[1,7744]{1,0:T(1,128)}, u32[]{:S(2)}) copy-start(f32[1,7744]{1,0:T(1,128)} %get-tuple-element.98) | copy-start | bytes 92932
  117.3 22.1 %copy-start.46 = (f32[1,7744]{1,0:T(1,128)S(1)}, f32[1,7744]{1,0:T(1,128)}, u32[]{:S(2)}) copy-start(f32[1,7744]{1,0:T(1,128)} %get-tuple-element.99) | copy-start | bytes 92932
  117.3 22.1 %copy-start.47 = (f32[1,7744]{1,0:T(1,128)S(1)}, f32[1,7744]{1,0:T(1,128)}, u32[]{:S(2)}) copy-start(f32[1,7744]{1,0:T(1,128)} %get-tuple-element.100) | copy-start | bytes 92932
  117.4 22.1 %copy-start.48 = (f32[1,7744]{1,0:T(1,128)S(1)}, f32[1,7744]{1,0:T(1,128)}, u32[]{:S(2)}) copy-start(f32[1,7744]{1,0:T(1,128)} %get-tuple-element.101) | copy-start | bytes 92932
  117.4 22.1 %copy-start.49 = (f32[1,7744]{1,0:T(1,128)S(1)}, f32[1,7744]{1,0:T(1,128)}, u32[]{:S(2)}) copy-start(f32[1,7744]{1,0:T(1,128)} %get-tuple-element.103) | copy-start | bytes 92932
  117.4 22.1 %copy-start.50 = (f32[1,7744]{1,0:T(1,128)S(1)}, f32[1,7744]{1,0:T(1,128)}, u32[]{:S(2)}) copy-start(f32[1,7744]{1,0:T(1,128)} %get-tuple-element.104) | copy-start | bytes 92932
  117.4 22.1 %copy-start.51 = (f32[1,7744]{1,0:T(1,128)S(1)}, f32[1,7744]{1,0:T(1,128)}, u32[]{:S(2)}) copy-start(f32[1,7744]{1,0:T(1,128)} %get-tuple-element.105) | copy-start | bytes 92932
  117.5 36.7 %all-to-all-start = ((f32[1,32,7786]{2,0,1:T(1,128)}), f32[1,32,7786]{2,0,1:T(1,128)}, u32[]{:S(2)}, u32[]{:S(2)}) async-start(f32[1,32,7786]{2,0,1:T(1,128)} %concatenate.13), calls=%async_computation | async-start | bytes 1998848 | tf_op jit(solution)/shard_map/all_to_all | solution.py:30
  142.4 36.7 %copy-start.16 = (f32[88,88,40]{1,0,2:T(8,128)}, f32[88,88,40]{1,0,2:T(8,128)S(1)}, u32[]{:S(2)}) copy-start(f32[88,88,40]{1,0,2:T(8,128)S(1)} %dot_general.209) | copy-start | bytes 3717124
  155.7 10.8 %all-to-all-start.3 = ((f32[1,32,2]{2,0,1:T(1,128)}), f32[1,32,2]{2,0,1:T(1,128)S(1)}, u32[]{:S(2)}, u32[]{:S(2)}) async-start(f32[1,32,2]{2,0,1:T(1,128)} %split.14), calls=%async_computation.3 | async-start | bytes 32768 | tf_op jit(solution)/shard_map/all_to_all | solution.py:142
  166.5 8.3 %all-to-all-start.1 = ((f32[8,1,160]{2,1,0:T(1,128)}), f32[8,1,160]{2,1,0:T(1,128)S(1)}, u32[]{:S(2)}, u32[]{:S(2)}) async-start(f32[8,1,160]{2,1,0:T(1,128)} %reshape.5389), calls=%async_computation.1 | async-start | bytes 16384 | tf_op jit(solution)/shard_map/all_to_all | solution.py:141
  174.8 37.2 %all-to-all-start.2 = ((f32[1,32,7744]{2,0,1:T(1,128)}), f32[1,32,7744]{2,0,1:T(1,128)S(1)}, u32[]{:S(2)}, u32[]{:S(2)}) async-start(f32[1,32,7744]{2,0,1:T(1,128)} %bitcast.441), calls=%async_computation.2 | async-start | bytes 1998848 | tf_op jit(solution)/shard_map/all_to_all | solution.py:140
  339.4 34.1 %copy-start.1 = (f32[1,32,40]{2,1,0:T(8,128)S(1)}, f32[1,32,40]{2,1,0:T(8,128)}, u32[]{:S(2)}) copy-start(f32[1,32,40]{2,1,0:T(8,128)} %param.7) | copy-start | bytes 15364
  343.0 10.1 %all-to-all-start.4 = ((f32[8,1,160]{2,1,0:T(1,128)}), f32[8,1,160]{2,1,0:T(1,128)S(1)}, u32[]{:S(2)}, u32[]{:S(2)}) async-start(f32[8,1,160]{2,1,0:T(1,128)} %reshape.5391), calls=%async_computation.4 | async-start | bytes 16384 | tf_op jit(solution)/shard_map/all_to_all | solution.py:221
  354.4 17.7 %all-to-all-start.5 = ((f32[1,32,40]{2,0,1:T(1,128)}), f32[1,32,40]{2,0,1:T(1,128)S(1)}, u32[]{:S(2)}, u32[]{:S(2)}) async-start(f32[1,32,40]{2,0,1:T(1,128)} %bitcast.45), calls=%async_computation.5 | async-start | bytes 32768 | tf_op jit(solution)/shard_map/all_to_all | solution.py:222
  (46 other events, 517.3 us)
where the time goes:
time: 381 us; the launch traced here: 374 us
  matrix products  145 us (38%)
  local copies, waits for them, and re-layouts  118 us (31%)
  other arithmetic  51.6 us (14%)
  starting transfers between devices  39.7 us (10%)
  waiting for transfers between devices  15.7 us (4%)
    gather x96, local copies, waits for them, and re-layouts  84.7 us
    dot_general x32, matrix products, apply_columns(): return jnp.einsum('vk,ukb->uvb', table, values, precision=highest)  67.1 us
    dot_general x30, matrix products, apply_rows(): return jnp.einsum('uk,kvb->uvb', table, values, precision=highest)  52.3 us
    mul x5, other arithmetic, zernike_table(): surfaces.append(surface * inside)  28.6 us
    dot_general x2, matrix products, shards(): jnp.dot(jnp.transpose(zernike_flat), jnp.transpose(current), precision=hi...  15.6 us
    all_to_all x1, starting transfers between devices, shards(): lax.all_to_all(finals, 'pat', split_axis=1, concat_axis=1, tiled=True)  12.1 us
    another operation x2, local copies, waits for them, and re-layouts, zernike_table(): return (jnp.stack(surfaces), inside)  11.9 us
    reduce_sum x6, other arithmetic, frame_total(): jnp.sum(values.reshape(PATCH, PATCH, frames_here, patches_here), axis=2)  10.2 us
  transfers between devices with their start and end apart: 7, of which 4 were waited for; matrix products, arithmetic and copies ran while one was open for 23% of the time, Pallas kernels for 0%

commit v1 on v0

v1 whole, which is shorter than its diff:
```python
import functools
import math

import jax
import jax.numpy as jnp
import ml_dtypes
import numpy as np
from jax import lax
from jax.experimental import pallas as pl
from jax.experimental.pallas import tpu as pltpu
from jax.sharding import PartitionSpec as P

N = 88
MODES = 40
ITERS = 2
FRAMES = 8
SH = 128
PPS = 32
GROUPS = 16
LOW = 22
NX = 45
XP = 24
NU = 45
ROWS = 184
DAMPING = 0.05
STEP = 64.0
f32, bf16 = jnp.float32, jnp.bfloat16
MESH = pl.DeviceIdType.MESH


def noll_index(j):
    n = 0
    remaining = j - 1
    while remaining > n:
        n += 1
        remaining -= n
    m = (-1) ** j * (n % 2 + 2 * ((remaining + (n + 1) % 2) // 2))
    return (n, m)


def zernike_values(row, col):
    radius = np.sqrt(row * row + col * col)
    angle = np.arctan2(row, col)
    values = []
    for j in range(2, MODES + 2):
        n, m = noll_index(j)
        k_abs = abs(m)
        radial = np.zeros_like(radius)
        for k in range((n - k_abs) // 2 + 1):
            factor = (
                (-1) ** k
                * math.factorial(n - k)
                / (
                    math.factorial(k)
                    * math.factorial((n + k_abs) // 2 - k)
                    * math.factorial((n - k_abs) // 2 - k)
                )
            )
            radial = radial + factor * radius ** (n - 2 * k)
        if m == 0:
            values.append(math.sqrt(n + 1) * radial)
        elif m > 0:
            values.append(math.sqrt(2 * (n + 1)) * radial * np.cos(k_abs * angle))
        else:
            values.append(math.sqrt(2 * (n + 1)) * radial * np.sin(k_abs * angle))
    return np.stack(values)


def ultraspherical(order, t):
    t = np.asarray(t, np.float64)
    inside = (np.arange(NX) + LOW - 44.0) / 22.0

    def raw(x):
        last, value = np.zeros_like(x), np.ones_like(x)
        for n in range(1, order + 1):
            last, value = value, (2.0 * (n + 2.0) * x * value - (n + 4.0) * last) / n
        return value

    weight = np.sqrt(1.0 - inside**2)
    return raw(t) / np.sqrt(np.sum(weight * raw(inside) ** 2) / np.sum(weight))


PAIRS = [(a, b) for a in range(9) for b in range(9 - a)]


def halves(table):
    hi = table.astype(np.float32).astype(ml_dtypes.bfloat16)
    lo = (table - hi.astype(np.float64)).astype(np.float32).astype(ml_dtypes.bfloat16)
    return hi, lo


def right_table(table):
    hi, lo = halves(table)
    return np.concatenate([hi, hi, lo], axis=0)


def left_table(table):
    hi, lo = halves(table)
    return np.concatenate([hi, hi, lo], axis=1)


@functools.lru_cache
def tables():
    w = 2.0 * np.pi / N
    full = np.arange(N)
    px = LOW + np.arange(NX)
    unit = (px - 44.0) / 22.0
    aperture = (unit[:, None] ** 2 + unit[None, :] ** 2 <= 1.0).astype(np.float64)
    a32 = ((px.astype(np.float32) - np.float32(44)) / np.float32(22)).astype(np.float32)
    r32 = np.sqrt(a32[:, None] * a32[:, None] + a32[None, :] * a32[None, :])
    assert np.array_equal(aperture, (r32 <= 1.0).astype(np.float64))
    scale = 1.0 / (N * N * aperture.sum())
    root = math.sqrt(scale)

    grid = np.linspace(-1.0, 1.0, 31)
    rows, cols = (g.ravel() for g in np.meshgrid(grid, grid, indexing="ij"))
    basis = np.stack([ultraspherical(a, rows) * ultraspherical(b, cols) for a, b in PAIRS], axis=1)
    fit = np.linalg.lstsq(basis, zernike_values(rows, cols).T, rcond=None)[0].T

    out = {}
    spread_ab = np.zeros((MODES, 128))
    spread_ab[:, : len(PAIRS)] = fit
    spread_ab[:, 64 : 64 + len(PAIRS)] = fit
    m1 = np.zeros((128, 128))
    m1[:MODES] = spread_ab
    out["m1"] = fine_table(m1)
    out["m2"] = fine_table(m1.T)

    along = np.zeros((XP, 128))
    mask = np.zeros((XP, 128))
    t3 = np.zeros((128, 128))
    for h in range(2):
        for k, (a, b) in enumerate(PAIRS):
            for i in range(XP):
                if i + XP * h < NX:
                    along[i, 64 * h + k] = ultraspherical(a, unit[i + XP * h])
            t3[64 * h + k, 64 * h : 64 * h + NX] = ultraspherical(b, unit)
        for i in range(XP):
            if i + XP * h < NX:
                mask[i, 64 * h : 64 * h + NX] = aperture[i + XP * h]
    out["along"] = np.repeat(along, FRAMES, axis=0).astype(np.float32)
    out["mask"] = np.repeat(mask, FRAMES, axis=0).astype(np.float32)
    out["t3"] = fine_table(t3)
    out["t18"] = fine_table(t3.T)

    ang = w * (np.outer(px, full) % N)
    c, s = np.cos(ang), np.sin(ang)
    for h in range(2):
        t5 = np.zeros((256, 256))
        lanes = slice(64 * h, 64 * h + NX)
        lanes2 = slice(128 + 64 * h, 128 + 64 * h + NX)
        t5[lanes, :N], t5[lanes2, :N] = c, s
        t5[lanes, 128 : 128 + N], t5[lanes2, 128 : 128 + N] = -s, c
        out[f"t5{h}"] = right_table(t5)
        t16 = np.zeros((256, 256))
        t16[:N, lanes], t16[128 : 128 + N, lanes] = c.T, -s.T
        t16[:N, lanes2], t16[128 : 128 + N, lanes2] = s.T, c.T
        out[f"t16{h}"] = right_table(t16)
    l7 = np.zeros((176, 96))
    l7[:N, :NX], l7[:N, 48 : 48 + NX] = c.T, s.T
    l7[N:, :NX], l7[N:, 48 : 48 + NX] = -s.T, c.T
    out["l7"] = left_table(l7 * root)
    l15 = np.zeros((96, 176))
    l15[:NX, :N], l15[:NX, N:] = c, -s
    l15[48 : 48 + NX, :N], l15[48 : 48 + NX, N:] = s, c
    out["l15"] = left_table(l15)

    ang = w * (np.outer(full, full) % N)
    c, s = np.cos(ang), np.sin(ang)
    t9 = np.zeros((128, 256))
    t9[:N, :N], t9[:N, 128 : 128 + N] = c, -s
    out["t9"] = right_table(t9)
    l10 = np.zeros((96, 176))
    l10[:NU, :N], l10[:NU, N:] = c[:NU], s[:NU]
    l10[48 : 48 + NU, :N], l10[48 : 48 + NU, N:] = -s[:NU], c[:NU]
    out["l10"] = left_table(l10)
    t12 = np.zeros((256, 256))
    t12[:N, :N], t12[128 : 128 + N, :N] = c, -s
    t12[:N, 128 : 128 + N], t12[128 : 128 + N, 128 : 128 + N] = s, c
    out["t12"] = right_table(t12)
    weight = np.full((NU,), 2.0)
    weight[0] = weight[44] = 1.0
    weight = weight * (-2.0) * 2.0 * root
    l13 = np.zeros((96, 96))
    l13[:N, :NU], l13[:N, 48 : 48 + NU] = c[:, :NU] * weight, -s[:, :NU] * weight
    out["l13"] = left_table(l13)

    profile = 0.5 - 0.5 * np.cos(2.0 * np.pi * (full + 0.5) / N)
    window = np.zeros((N, 128), np.float32)
    window[:, :N] = profile[:, None] * profile[None, :]
    out["window"] = window
    signed = (full + 44) % N - 44.0
    freq = np.zeros((2, 48, 128), np.float32)
    freq[0, :NU, :] = signed[:NU, None]
    freq[1, :, :N] = signed[None, :]
    out["freq"] = (freq * (-w)).astype(np.float32)

    flip = np.zeros((128, 128), ml_dtypes.bfloat16)
    for v in range(N):
        flip[(N - v) % N, v] = 1
    out["flip"] = np.concatenate([flip, flip], axis=0)
    place = np.zeros((176, 192), ml_dtypes.bfloat16)
    for u in range(N):
        if u < NU:
            place[u, u] = 1
            place[N + u, 48 + u] = 1
        else:
            place[u, 96 + N - u] = 1
            place[N + u, 144 + N - u] = -1
    out["place"] = np.concatenate([place, place], axis=1)
    return out


def fine_table(table):
    hi = table.astype(np.float32).astype(ml_dtypes.bfloat16)
    rest = table - hi.astype(np.float64)
    mid = rest.astype(np.float32).astype(ml_dtypes.bfloat16)
    low = (rest - mid.astype(np.float64)).astype(np.float32).astype(ml_dtypes.bfloat16)
    return np.concatenate([hi, hi, mid, mid, low, hi], axis=0)


def split(x):
    hi = x.astype(bf16)
    return hi, (x - hi.astype(f32)).astype(bf16)


def dot(a, b):
    return jnp.dot(a, b, preferred_element_type=f32)


def right(x, table):
    hi, lo = split(x)
    return dot(jnp.concatenate([hi, lo, hi], axis=1), table)


def fine(x, table):
    hi = x.astype(bf16)
    rest = x - hi.astype(f32)
    mid = rest.astype(bf16)
    low = (rest - mid.astype(f32)).astype(bf16)
    return dot(jnp.concatenate([hi, mid, hi, mid, hi, low], axis=1), table)


def left(table, x):
    hi, lo = split(x)
    return dot(table, jnp.concatenate([hi, lo, hi], axis=0))


def sincos(x):
    k = jnp.floor(x * (2.0 / math.pi) + 0.5)
    r = x - k * 1.5703125
    r = r - k * 4.8351287841796875e-4
    r = r - k * 3.1385570764541626e-07
    z = r * r
    s = r + r * z * (-1.6666654611e-1 + z * (8.3321608736e-3 + z * -1.9515295891e-4))
    c = 1.0 - 0.5 * z + z * z * (
        4.166664568298827e-2 + z * (-1.388731625493765e-3 + z * 2.443315711809948e-5)
    )
    q = k.astype(jnp.int32)
    swap = (q & 1) == 1
    sin = jnp.where(swap, c, s)
    cos = jnp.where(swap, s, c)
    sin = jnp.where((q & 2) == 2, -sin, sin)
    cos = jnp.where(((q + 1) & 2) == 2, -cos, cos)
    return sin, cos


NAMES = (
    "m1",
    "m2",
    "along",
    "mask",
    "t3",
    "t18",
    "t50",
    "t51",
    "t160",
    "t161",
    "l7",
    "l15",
    "t9",
    "l10",
    "t12",
    "l13",
    "window",
    "freq",
    "flip",
    "place",
)


def maths_kernel(recv, *refs):
    tab = dict(zip(NAMES, refs[: len(NAMES)]))
    new_ref, obj_ref = refs[len(NAMES) : len(NAMES) + 2]
    ramp, ysc, foc, asc, dat, tra, gsc, hsc, pup = refs[len(NAMES) + 2 :]
    j = pl.program_id(0)
    which = lax.rem(j, 2)

    def half_spectra(values):
        asc[...] = right(values, tab["t9"][...])
        for f in range(0, FRAMES, 2):
            stacked = []
            for g in (f, f + 1):
                part = asc[g * N : (g + 1) * N, :]
                stacked.append(jnp.concatenate([part[:, :128], part[:, 128:]], axis=0))
            out = left(tab["l10"][...], jnp.concatenate(stacked, axis=1))
            yield f, out[:, :128]
            yield f + 1, out[:, 128:]

    @pl.when(j == 0)
    def _():
        for f in range(FRAMES):
            angle = (
                tab["freq"][0] * recv[0, f, 178:179, :] + tab["freq"][1] * recv[0, f, 179:180, :]
            )
            sin, cos = sincos(angle)
            ramp[f, 0] = cos
            ramp[f, 1] = sin

    energy = []
    window = tab["window"][...]
    parts = []
    lane = lax.broadcasted_iota(jnp.int32, (N, 128), 1)
    start = pl.multiple_of(which * N, 8)
    total = jnp.zeros((N, 128), f32)
    for f in range(FRAMES):
        part = jnp.where(lane < N, recv[0, f, pl.ds(start, N), :], 0.0) * window
        total = total + part * part
        parts.append(part)
    energy = jnp.sum(total) * float(N * N)
    for f, out in half_spectra(jnp.concatenate(parts, axis=0)):
        re, im = out[:48], out[48:]
        cos, sin = ramp[f, 0], ramp[f, 1]
        dat[f, :48] = re * cos - im * sin
        dat[f, 48:] = re * sin + im * cos
    rows = [recv[0, f, pl.ds(176 + which, 1), :] for f in range(FRAMES)]
    lane8 = lax.broadcasted_iota(jnp.int32, (FRAMES, 128), 1)
    current = jnp.where(lane8 < MODES, jnp.concatenate(rows, axis=0), 0.0)
    step = (STEP * FRAMES) / (jnp.zeros((FRAMES, 128), f32) + energy)

    def iterate(_, current):
        cab = fine(current, tab["m1"][...])
        along = tab["along"][...]
        phase = fine(jnp.concatenate([cab] * XP, axis=0) * along, tab["t3"][...])
        sin, cos = sincos(phase)
        mask = tab["mask"][...]
        pr, pi = cos * mask, sin * mask
        pup[0] = pr
        pup[1] = pi
        hi, lo = split(jnp.concatenate([pr, pi], axis=1))
        stack = jnp.concatenate([hi, lo, hi], axis=1)
        for h in range(2):
            out = dot(stack, tab[f"t5{h}"][...])
            ysc[h] = out[:, :128]
            ysc[2 + h] = out[:, 128:]
        spreads = []
        for f in range(0, FRAMES, 2):
            both = []
            for g in (f, f + 1):
                both.append(
                    jnp.concatenate([ysc[h, pl.ds(g, XP, FRAMES), :] for h in range(4)], axis=0)
                )
            out = left(tab["l7"][...], jnp.concatenate(both, axis=1))
            for g in (0, 1):
                one = out[:, 128 * g : 128 * g + 128]
                foc[f + g] = one
                spreads.append(one[:N] * one[:N] + one[N:] * one[N:])
        cre = jnp.zeros((48, 128), f32)
        cim = jnp.zeros((48, 128), f32)
        den = jnp.full((48, 128), DAMPING, f32)
        for f, out in half_spectra(jnp.concatenate(spreads, axis=0)):
            tra[f] = out
            tre, tim = out[:48], out[48:]
            dre, dim = dat[f, :48], dat[f, 48:]
            cre = cre + (dre * tre + dim * tim)
            cim = cim + (dim * tre - dre * tim)
            den = den + (tre * tre + tim * tim)
        ere, eim = cre / den, cim / den
        obj_ref[0, 0, :48] = ere
        obj_ref[0, 1, :48] = eim
        for f in range(FRAMES):
            tre, tim = tra[f, :48], tra[f, 48:]
            mre = dat[f, :48] - (ere * tre - eim * tim)
            mim = dat[f, 48:] - (ere * tim + eim * tre)
            gsc[f * 48 : f * 48 + 48, :128] = ere * mre + eim * mim
            gsc[f * 48 : f * 48 + 48, 128:] = ere * mim - eim * mre
        gsc[...] = right(gsc[...], tab["t12"][...])
        for f in range(0, FRAMES, 2):
            both = []
            for g in (f, f + 1):
                part = gsc[g * 48 : g * 48 + 48, :]
                both.append(jnp.concatenate([part[:, :128], part[:, 128:]], axis=0))
            grad = left(tab["l13"][...], jnp.concatenate(both, axis=1))[:N]
            both = []
            for g in (0, 1):
                one = grad[:, 128 * g : 128 * g + 128]
                both.append(
                    jnp.concatenate([one * foc[f + g, :N], one * foc[f + g, N:]], axis=0)
                )
            out = left(tab["l15"][...], jnp.concatenate(both, axis=1))
            for g in (0, 1):
                re, im = (out[k : k + 48, 128 * g : 128 * g + 128] for k in (0, 48))
                for h in range(2):
                    rows = slice(XP * h, XP * h + XP)
                    hsc[2 * h, pl.ds(f + g, XP, FRAMES), :] = re[rows]
                    hsc[2 * h + 1, pl.ds(f + g, XP, FRAMES), :] = im[rows]
        back = None
        for h in range(2):
            out = right(
                jnp.concatenate([hsc[2 * h], hsc[2 * h + 1]], axis=1), tab[f"t16{h}"][...]
            )
            back = out if back is None else back + out
        grad = back[:, 128:] * pup[0] - back[:, :128] * pup[1]
        gab = fine(grad, tab["t18"][...]) * tab["along"][...]
        acc = gab[:FRAMES]
        for i in range(1, XP):
            acc = acc + gab[i * FRAMES : (i + 1) * FRAMES]
        return current - step * fine(acc, tab["m2"][...])

    new_ref[0] = lax.fori_loop(0, ITERS, iterate, current)
    half = jnp.concatenate([obj_ref[0, 0, :48], obj_ref[0, 1, :48]], axis=0) * (1.0 / N)
    hi, lo = split(half)
    flipped = dot(jnp.concatenate([hi, lo], axis=1), tab["flip"][...])
    hi, lo = split(jnp.concatenate([half, flipped], axis=0))
    out = dot(tab["place"][...], jnp.concatenate([hi, lo], axis=0))
    obj_ref[0, 0] = out[:N]
    obj_ref[0, 1] = out[N:]


def maths(recv):
    consts = [jnp.asarray(tables()[name]) for name in NAMES]
    whole = [
        pl.BlockSpec(c.shape, functools.partial(lambda d, j: (0,) * d, c.ndim)) for c in consts
    ]
    return pl.pallas_call(
        maths_kernel,
        grid=(4,),
        in_specs=[pl.BlockSpec((1, FRAMES, ROWS, 128), lambda j: (j // 2, 0, 0, 0))] + whole,
        out_specs=[
            pl.BlockSpec((1, FRAMES, 128), lambda j: (j, 0, 0)),
            pl.BlockSpec((1, 2, N, 128), lambda j: (j, 0, 0, 0)),
        ],
        out_shape=[
            jax.ShapeDtypeStruct((4, FRAMES, 128), f32),
            jax.ShapeDtypeStruct((4, 2, N, 128), f32),
        ],
        scratch_shapes=[
            pltpu.VMEM((FRAMES, 2, 48, 128), f32),
            pltpu.VMEM((4, XP * FRAMES, 128), f32),
            pltpu.VMEM((FRAMES, 176, 128), f32),
            pltpu.VMEM((FRAMES * N, 256), f32),
            pltpu.VMEM((FRAMES, 96, 128), f32),
            pltpu.VMEM((FRAMES, 96, 128), f32),
            pltpu.VMEM((FRAMES * 48, 256), f32),
            pltpu.VMEM((4, XP * FRAMES, 128), f32),
            pltpu.VMEM((2, XP * FRAMES, 128), f32),
        ],
        compiler_params=pltpu.CompilerParams(vmem_limit_bytes=48 << 20),
        name="maths",
    )(recv, *consts)


def pair_counts(me_pat, me_frm):
    return lax.div(me_pat, 2) == me_frm


def exchange_kernel(
    frames,
    shifts,
    coefs,
    anchors,
    assign,
    recv,
    strip,
    send,
    load_sem,
    halo_send,
    halo_recv,
    send_sem,
    recv_sem,
    own_sem,
):
    me_frm, me_pat = lax.axis_index("frm"), lax.axis_index("pat")
    target = lax.div(me_pat, 2)
    side = lax.rem(me_pat, 2)
    own = pair_counts(me_pat, me_frm)

    def load(t):
        return pltpu.make_async_copy(
            frames.at[0, :, pl.ds(pl.multiple_of(t * 128, 128), 128)],
            strip.at[t, pl.ds(0, SH), :],
            load_sem.at[t],
        )

    def start_load(t, _):
        load(t).start()
        return 0

    lax.fori_loop(0, 16, start_load, 0)

    barrier = pltpu.get_barrier_semaphore()

    def greet(q, _):
        pat, frm = 2 * me_frm + lax.div(q, 8), lax.rem(q, 8)

        @pl.when(jnp.logical_not((pat == me_pat) & (frm == me_frm)))
        def _():
            pl.semaphore_signal(
                barrier, inc=1, device_id={"frm": frm, "pat": pat}, device_id_type=MESH
            )

        return 0

    lax.fori_loop(0, 16, greet, 0)

    @pl.when(me_pat < GROUPS - 1)
    def _():
        pl.semaphore_signal(
            barrier, inc=1, device_id={"frm": me_frm, "pat": me_pat + 1}, device_id_type=MESH
        )

    send[:, 176:, :] = jnp.zeros((GROUPS, 8, 128), f32)

    @pl.when(me_pat == GROUPS - 1)
    def _():
        strip[:, SH:, :] = jnp.zeros((16, N, 128), f32)

    def end_load(t, _):
        load(t).wait()
        return 0

    lax.fori_loop(0, 16, end_load, 0)
    pl.semaphore_wait(
        barrier, 16 - own.astype(jnp.int32) + (me_pat > 0).astype(jnp.int32)
    )

    def halo():
        return pltpu.make_async_remote_copy(
            src_ref=strip.at[:, pl.ds(0, N), :],
            dst_ref=strip.at[:, pl.ds(SH, N), :],
            send_sem=halo_send,
            recv_sem=halo_recv,
            device_id={"frm": me_frm, "pat": jnp.maximum(me_pat - 1, 0)},
            device_id_type=MESH,
        )

    @pl.when(me_pat > 0)
    def _():
        halo().start()

    @pl.when(me_pat < GROUPS - 1)
    def _():
        halo().wait_recv()

    lane = lax.broadcasted_iota(jnp.int32, (N, 128), 1)
    top = me_pat * SH

    def message(g):
        return pltpu.make_async_remote_copy(
            src_ref=send.at[g],
            dst_ref=recv.at[side, me_frm],
            send_sem=send_sem.at[g],
            recv_sem=recv_sem.at[side * 8 + me_frm],
            device_id={"frm": target, "pat": g},
            device_id_type=MESH,
        )

    def own_message():
        return pltpu.make_async_copy(send.at[me_pat], recv.at[side, me_frm], own_sem)

    def fill(i, _):
        g = lax.rem(me_pat + 1 + i, GROUPS)
        first = jnp.int32(0)
        second = jnp.int32(0)
        for p in range(PPS - 1, -1, -1):
            hit = assign[p] == g
            second = jnp.where(hit, first, second)
            first = jnp.where(hit, p, first)
        for k, p in enumerate((first, second)):
            row = jnp.clip(anchors[p, 0] - top, 0, SH - 1)
            col = anchors[p, 1]
            tile = jnp.clip(lax.shift_right_logical(col, 7), 0, 15)
            off = col & 127
            a = strip[tile, pl.ds(row, N), :]
            b = strip[jnp.minimum(tile + 1, 15), pl.ds(row, N), :]
            turn = (128 - off) & 127
            cut = jnp.where(
                lane < 128 - off, pltpu.roll(a, turn, 1), pltpu.roll(b, turn, 1)
            )
            send[g, k * N : k * N + N, :] = cut
            send[g, 176 + k : 177 + k, :MODES] = coefs[0, pl.ds(p, 1), :]
            send[g, 178 + k : 179 + k, :] = jnp.zeros((1, 128), f32) + shifts[0, k]
        me = own & (g == me_pat)

        @pl.when(jnp.logical_not(me))
        def _():
            message(g).start()

        @pl.when(me)
        def _():
            own_message().start()

        return 0

    lax.fori_loop(0, GROUPS, fill, 0)

    def finish(q, _):
        me = own & (q == me_pat)

        @pl.when(jnp.logical_not(me))
        def _():
            message(q).wait_send()

        @pl.when(me)
        def _():
            own_message().wait()

        pat, frm = 2 * me_frm + lax.div(q, 8), lax.rem(q, 8)

        @pl.when(jnp.logical_not((pat == me_pat) & (frm == me_frm)))
        def _():
            pltpu.make_async_remote_copy(
                src_ref=send.at[q],
                dst_ref=recv.at[lax.div(q, 8), frm],
                send_sem=send_sem.at[q],
                recv_sem=recv_sem.at[q],
                device_id={"frm": frm, "pat": pat},
                device_id_type=MESH,
            ).wait_recv()

        return 0

    lax.fori_loop(0, GROUPS, finish, 0)

    @pl.when(me_pat > 0)
    def _():
        halo().wait_send()


def exchange(frames, shifts, coefficients, anchors, assign):
    smem = pl.BlockSpec(memory_space=pltpu.SMEM)
    return pl.pallas_call(
        exchange_kernel,
        in_specs=[
            pl.BlockSpec(memory_space=pl.ANY),
            smem,
            pl.BlockSpec(memory_space=pltpu.VMEM),
            smem,
            smem,
        ],
        out_specs=pl.BlockSpec(memory_space=pl.ANY),
        out_shape=jax.ShapeDtypeStruct((2, FRAMES, ROWS, 128), f32),
        scratch_shapes=[
            pltpu.VMEM((16, SH + N, 128), f32),
            pltpu.VMEM((GROUPS, ROWS, 128), f32),
            pltpu.SemaphoreType.DMA((16,)),
            pltpu.SemaphoreType.DMA,
            pltpu.SemaphoreType.DMA,
            pltpu.SemaphoreType.DMA((GROUPS,)),
            pltpu.SemaphoreType.DMA((GROUPS,)),
            pltpu.SemaphoreType.DMA,
        ],
        compiler_params=pltpu.CompilerParams(
            collective_id=0, has_side_effects=True, vmem_limit_bytes=32 << 20
        ),
        name="exchange",
    )(frames, shifts, coefficients, anchors, assign)


def back_kernel(new, assign, out, send, recv, place, send_sem, recv_sem, own_sem):
    me_frm, me_pat = lax.axis_index("frm"), lax.axis_index("pat")
    target = lax.div(me_pat, 2)
    side = lax.rem(me_pat, 2)
    own = pair_counts(me_pat, me_frm)
    barrier = pltpu.get_barrier_semaphore()

    def greet(g, _):
        @pl.when(jnp.logical_not(own & (g == me_pat)))
        def _():
            pl.semaphore_signal(
                barrier, inc=1, device_id={"frm": target, "pat": g}, device_id_type=MESH
            )

        return 0

    lax.fori_loop(0, GROUPS, greet, 0)
    send[...] = jnp.zeros((16, 8, 128), f32)
    for k in range(2):
        for f in range(FRAMES):
            for i in range(2):
                send[k * 8 + f, i : i + 1, :] = new[2 * k + i, f : f + 1, :]
    pl.semaphore_wait(barrier, 16 - own.astype(jnp.int32))

    def message(q):
        return pltpu.make_async_remote_copy(
            src_ref=send.at[q],
            dst_ref=recv.at[me_pat],
            send_sem=send_sem.at[q],
            recv_sem=recv_sem.at[me_pat],
            device_id={"frm": lax.rem(q, 8), "pat": 2 * me_frm + lax.div(q, 8)},
            device_id_type=MESH,
        )

    here = side * 8 + me_frm

    def own_message():
        return pltpu.make_async_copy(send.at[here], recv.at[me_pat], own_sem)

    def start(q, _):
        me = own & (q == here)

        @pl.when(jnp.logical_not(me))
        def _():
            message(q).start()

        @pl.when(me)
        def _():
            own_message().start()

        return 0

    lax.fori_loop(0, 16, start, 0)

    def count(p, _):
        mine = assign[p]
        seen = jnp.int32(0)
        for q in range(PPS):
            seen = seen + jnp.where((assign[q] == mine) & (q < p), 1, 0)
        place[p] = jnp.clip(seen, 0, 1)
        return 0

    lax.fori_loop(0, PPS, count, 0)

    def finish(q, _):
        me = own & (q == here)

        @pl.when(jnp.logical_not(me))
        def _():
            message(q).wait_send()

        @pl.when(me)
        def _():
            own_message().wait()

        @pl.when(jnp.logical_not(own & (q == me_pat)))
        def _():
            pltpu.make_async_remote_copy(
                src_ref=send.at[q],
                dst_ref=recv.at[q],
                send_sem=send_sem.at[q],
                recv_sem=recv_sem.at[q],
                device_id={"frm": target, "pat": q},
                device_id_type=MESH,
            ).wait_recv()

        return 0

    lax.fori_loop(0, 16, finish, 0)
    for p in range(PPS):
        out[0, p : p + 1, :] = recv[assign[p], pl.ds(place[p], 1), :][:, :MODES]


def give_back(new, assign):
    return pl.pallas_call(
        back_kernel,
        in_specs=[
            pl.BlockSpec(memory_space=pltpu.VMEM),
            pl.BlockSpec(memory_space=pltpu.SMEM),
        ],
        out_specs=pl.BlockSpec(memory_space=pltpu.VMEM),
        out_shape=jax.ShapeDtypeStruct((1, PPS, MODES), f32),
        scratch_shapes=[
            pltpu.VMEM((16, 8, 128), f32),
            pltpu.VMEM((16, 8, 128), f32),
            pltpu.SMEM((PPS,), jnp.int32),
            pltpu.SemaphoreType.DMA((16,)),
            pltpu.SemaphoreType.DMA((16,)),
            pltpu.SemaphoreType.DMA,
        ],
        compiler_params=pltpu.CompilerParams(collective_id=1, has_side_effects=True),
        name="give_back",
    )(new, assign)


def shards(frames, shifts, coefficients, anchors, assign):
    recv = exchange(frames, shifts, coefficients, anchors, assign)
    new, spectra = maths(recv)
    coefs = give_back(new, assign)
    return coefs, spectra[:, :, :, :N].reshape(4, 2, N * N)


def solution(mesh):
    in_specs = (
        P("frm", "pat", None),
        P("frm", None),
        P("frm", "pat", None),
        P("pat", None),
        P("pat"),
    )
    out_specs = (P("frm", "pat", None), P(("pat", "frm"), None, None))
    return jax.shard_map(shards, mesh=mesh, in_specs=in_specs, out_specs=out_specs, check_vma=False)
```

time: 381 us -> 122 us (0.32)
  the two profiles are of different devices: /device:TPU:7 before, /device:TPU:25 now
where the time goes in v1:
time: 122 us
  Pallas kernels  104 us (85%)
  local copies, waits for them, and re-layouts  16.9 us (14%)
    pallas_call x1, Pallas kernels, exchange(): pl.pallas_call(exchange_kernel, in_specs=[pl.BlockSpec(memory_space=pl.AN...  51.7 us
    pallas_call x1, Pallas kernels, maths(): pl.pallas_call(maths_kernel, grid=(4,), in_specs=[pl.BlockSpec((1, FRAMES...  37.2 us
    unnamed x52, local copies, waits for them, and re-layouts  15.8 us
    pallas_call x1, Pallas kernels, give_back(): pl.pallas_call(back_kernel, in_specs=[pl.BlockSpec(memory_space=pltpu.VME...  15 us

profile of v1, /device:TPU:25, one launch (start us, length us, event | category | flops | bytes accessed | tf_op | source)
XLA Modules:
  0.0 121.6 jit_solution(153152186094075694)
XLA Ops:
  0.6 0.0 copy-start.19
  0.6 0.8 copy.27.anchors
  1.4 1.2 %copy-done = f32[1,128,2048]{2,1,0:T(8,128)S(1)} copy-done((f32[1,128,2048]{2,1,0:T(8,128)S(1)}, f32[1,128,2048]{2,1,0:T(8,128)}, u32[]{:S(2)}) %copy-start) | copy-done | bytes 1048600
  2.6 0.7 copy-done.21
  3.4 0.7 copy-done.23
  4.0 0.7 copy-done.24
  4.7 0.0 copy-start.5
  4.7 0.0 copy-start.6
  4.7 0.0 copy-start.7
  4.7 0.0 copy-start.8
  4.7 51.7 %exchange.1.recv = f32[2,8,184,128]{3,2,1,0:T(8,128)S(1)} custom-call(f32[1,128,2048]{2,1,0:T(8,128)S(1)} %copy-done, f32[1,2]{1,0:T(1,128)S(1)} %copy-done.24, f32[1,32,40]{2,1,0:T(8,128)S(1)} %copy-done.21, s32[32,2]{1,0:T(8,128)S(1)} %copy.27.anchors, s32[32]{0:T(128)S(1)} %copy-done.23), custom_call_target="tpu_custom_call" | custom-call | tf_op jit(solution)/shard_map/exchange/pallas_call | solution.py:642
  56.4 0.0 copy-done.19
  56.4 0.0 copy-done.1
  56.4 0.0 copy-done.2
  56.5 0.0 copy-start.9
  56.5 0.9 copy-done.9
  57.4 0.9 copy-done.10
  58.3 0.9 copy-done.11
  59.2 0.9 copy-done.12
  60.2 0.9 copy-done.13
  61.1 0.9 copy-done.14
  62.0 0.9 copy-done.15
  62.9 0.9 copy-done.16
  63.7 0.9 copy-done.17
  64.6 0.8 copy-done.18
  65.5 0.8 copy-done.20
  66.3 37.2 %maths.1 = (f32[4,8,128]{2,1,0:T(8,128)S(1)}, f32[4,2,88,128]{3,2,1,0:T(8,128)S(1)}) custom-call(f32[2,8,184,128]{3,2,1,0:T(8,128)S(1)} %exchange.1.recv, bf16[768,128]{1,0:T(8,128)(2,1)S(1)} %copy-done.10, bf16[768,128]{1,0:T(8,128)(2,1)S(1)} %copy-done.9, f32[192,128]{1,0:T(8,128)S(1)} %copy-done.16, f32[192,128]{1,0:T(8,128)S(1)} %copy-done.15, ...), custom_call_target="tpu_custom_call" | custom-call | tf_op jit(solution)/shard_map/maths/pallas_call | solution.py:435
  103.5 0.0 copy-start.22
  103.5 0.6 copy-done.22
  104.1 15.0 %give_back.1 = f32[1,32,40]{2,1,0:T(8,128)} custom-call(f32[4,8,128]{2,1,0:T(8,128)} %copy-done.22, s32[32]{0:T(128)} %assign.3), custom_call_target="tpu_custom_call" | custom-call | tf_op jit(solution)/shard_map/give_back/pallas_call | solution.py:764
  119.1 1.1 reshape.7
  120.2 1.3 %copy.29 = f32[1,32,40]{2,1,0:T(8,128)} copy(f32[1,32,40]{2,1,0:T(8,128)} %give_back.1) | data formatting | bytes 10240
  (24 shorter events, 0.0 us)
Async XLA Ops:
  0.6 55.8 %copy-start.19 = (f32[2,48,128]{2,1,0:T(8,128)S(1)}, f32[2,48,128]{2,1,0:T(8,128)}, u32[]{:S(2)}) copy-start(f32[2,48,128]{2,1,0:T(8,128)} %constant.57.clone.refs_17_) | copy-start | bytes 147460
  1.4 1.2 %copy-start = (f32[1,128,2048]{2,1,0:T(8,128)S(1)}, f32[1,128,2048]{2,1,0:T(8,128)}, u32[]{:S(2)}) copy-start(f32[1,128,2048]{2,1,0:T(8,128)} %frames.1) | copy-start | bytes 3145732
  2.6 0.7 copy-start.21
  3.4 0.7 copy-start.23
  4.0 0.7 copy-start.24
  4.7 51.7 %copy-start.1 = (bf16[768,256]{1,0:T(8,128)(2,1)S(1)}, bf16[768,256]{1,0:T(8,128)(2,1)}, u32[]{:S(2)}) copy-start(bf16[768,256]{1,0:T(8,128)(2,1)} %constant.54.clone.refs_14_) | copy-start | bytes 1179652
  4.7 51.7 %copy-start.2 = (bf16[768,256]{1,0:T(8,128)(2,1)S(1)}, bf16[768,256]{1,0:T(8,128)(2,1)}, u32[]{:S(2)}) copy-start(bf16[768,256]{1,0:T(8,128)(2,1)} %constant.49.clone.refs_9_) | copy-start | bytes 1179652
  4.7 51.7 %copy-start.3 = (bf16[768,256]{1,0:T(8,128)(2,1)S(1)}, bf16[768,256]{1,0:T(8,128)(2,1)}, u32[]{:S(2)}) copy-start(bf16[768,256]{1,0:T(8,128)(2,1)} %constant.48.clone.refs_8_) | copy-start | bytes 1179652
  4.7 51.8 %copy-start.4 = (bf16[768,256]{1,0:T(8,128)(2,1)S(1)}, bf16[768,256]{1,0:T(8,128)(2,1)}, u32[]{:S(2)}) copy-start(bf16[768,256]{1,0:T(8,128)(2,1)} %constant.47.clone.refs_7_) | copy-start | bytes 1179652
  4.7 51.8 %copy-start.5 = (bf16[768,256]{1,0:T(8,128)(2,1)S(1)}, bf16[768,256]{1,0:T(8,128)(2,1)}, u32[]{:S(2)}) copy-start(bf16[768,256]{1,0:T(8,128)(2,1)} %constant.46.clone.refs_6_) | copy-start | bytes 1179652
  4.7 51.8 %copy-start.6 = (bf16[384,256]{1,0:T(8,128)(2,1)S(1)}, bf16[384,256]{1,0:T(8,128)(2,1)}, u32[]{:S(2)}) copy-start(bf16[384,256]{1,0:T(8,128)(2,1)} %constant.52.clone.refs_12_) | copy-start | bytes 589828
  4.7 51.8 %copy-start.7 = (bf16[768,128]{1,0:T(8,128)(2,1)S(1)}, bf16[768,128]{1,0:T(8,128)(2,1)}, u32[]{:S(2)}) copy-start(bf16[768,128]{1,0:T(8,128)(2,1)} %constant.45.clone.refs_5_) | copy-start | bytes 589828
  4.7 51.8 %copy-start.8 = (bf16[768,128]{1,0:T(8,128)(2,1)S(1)}, bf16[768,128]{1,0:T(8,128)(2,1)}, u32[]{:S(2)}) copy-start(bf16[768,128]{1,0:T(8,128)(2,1)} %constant.44.clone.refs_4_) | copy-start | bytes 589828
  56.5 0.9 copy-start.9
  57.4 0.9 copy-start.10
  58.3 0.9 copy-start.11
  59.2 0.9 copy-start.12
  60.2 0.9 copy-start.13
  61.1 0.9 copy-start.14
  62.0 0.9 copy-start.15
  62.8 0.9 copy-start.16
  63.7 0.9 copy-start.17
  64.6 0.8 copy-start.18
  65.5 0.8 copy-start.20
  103.5 0.6 copy-start.22

commit v2 on v0

v2 whole, which is shorter than its diff:
```python
import functools
import math

import jax
import jax.numpy as jnp
import ml_dtypes
import numpy as np
from jax import lax
from jax.experimental import pallas as pl
from jax.experimental.pallas import tpu as pltpu
from jax.sharding import PartitionSpec as P

N = 88
MODES = 40
ITERS = 2
FRAMES = 8
SH = 128
PPS = 32
GROUPS = 16
LOW = 22
NX = 45
XP = 24
NU = 45
PER = 4
DAMPING = 0.05
STEP = 64.0
f32, bf16 = jnp.float32, jnp.bfloat16
MESH = pl.DeviceIdType.MESH


def noll_index(j):
    n = 0
    remaining = j - 1
    while remaining > n:
        n += 1
        remaining -= n
    m = (-1) ** j * (n % 2 + 2 * ((remaining + (n + 1) % 2) // 2))
    return (n, m)


def zernike_values(row, col):
    radius = np.sqrt(row * row + col * col)
    angle = np.arctan2(row, col)
    values = []
    for j in range(2, MODES + 2):
        n, m = noll_index(j)
        k_abs = abs(m)
        radial = np.zeros_like(radius)
        for k in range((n - k_abs) // 2 + 1):
            factor = (
                (-1) ** k
                * math.factorial(n - k)
                / (
                    math.factorial(k)
                    * math.factorial((n + k_abs) // 2 - k)
                    * math.factorial((n - k_abs) // 2 - k)
                )
            )
            radial = radial + factor * radius ** (n - 2 * k)
        if m == 0:
            values.append(math.sqrt(n + 1) * radial)
        elif m > 0:
            values.append(math.sqrt(2 * (n + 1)) * radial * np.cos(k_abs * angle))
        else:
            values.append(math.sqrt(2 * (n + 1)) * radial * np.sin(k_abs * angle))
    return np.stack(values)


def ultraspherical(order, t):
    t = np.asarray(t, np.float64)
    inside = (np.arange(NX) + LOW - 44.0) / 22.0

    def raw(x):
        last, value = np.zeros_like(x), np.ones_like(x)
        for n in range(1, order + 1):
            last, value = value, (2.0 * (n + 2.0) * x * value - (n + 4.0) * last) / n
        return value

    weight = np.sqrt(1.0 - inside**2)
    return raw(t) / np.sqrt(np.sum(weight * raw(inside) ** 2) / np.sum(weight))


PAIRS = [(a, b) for a in range(9) for b in range(9 - a)]


def halves(table):
    hi = table.astype(np.float32).astype(ml_dtypes.bfloat16)
    lo = (table - hi.astype(np.float64)).astype(np.float32).astype(ml_dtypes.bfloat16)
    return hi, lo


def right_table(table):
    hi, lo = halves(table)
    return np.concatenate([hi, hi, lo], axis=0)


def left_table(table):
    hi, lo = halves(table)
    return np.concatenate([hi, hi, lo], axis=1)


@functools.lru_cache
def tables():
    w = 2.0 * np.pi / N
    full = np.arange(N)
    px = LOW + np.arange(NX)
    unit = (px - 44.0) / 22.0
    aperture = (unit[:, None] ** 2 + unit[None, :] ** 2 <= 1.0).astype(np.float64)
    a32 = ((px.astype(np.float32) - np.float32(44)) / np.float32(22)).astype(np.float32)
    r32 = np.sqrt(a32[:, None] * a32[:, None] + a32[None, :] * a32[None, :])
    assert np.array_equal(aperture, (r32 <= 1.0).astype(np.float64))
    scale = 1.0 / (N * N * aperture.sum())
    root = math.sqrt(scale)

    grid = np.linspace(-1.0, 1.0, 31)
    rows, cols = (g.ravel() for g in np.meshgrid(grid, grid, indexing="ij"))
    basis = np.stack([ultraspherical(a, rows) * ultraspherical(b, cols) for a, b in PAIRS], axis=1)
    fit = np.linalg.lstsq(basis, zernike_values(rows, cols).T, rcond=None)[0].T

    out = {}
    spread_ab = np.zeros((MODES, 128))
    spread_ab[:, : len(PAIRS)] = fit
    spread_ab[:, 64 : 64 + len(PAIRS)] = fit
    m1 = np.zeros((128, 128))
    m1[:MODES] = spread_ab
    out["m1"] = fine_table(m1)
    out["m2"] = fine_table(m1.T)

    along = np.zeros((XP, 128))
    mask = np.zeros((XP, 128))
    t3 = np.zeros((128, 128))
    for h in range(2):
        for k, (a, b) in enumerate(PAIRS):
            for i in range(XP):
                if i + XP * h < NX:
                    along[i, 64 * h + k] = ultraspherical(a, unit[i + XP * h])
            t3[64 * h + k, 64 * h : 64 * h + NX] = ultraspherical(b, unit)
        for i in range(XP):
            if i + XP * h < NX:
                mask[i, 64 * h : 64 * h + NX] = aperture[i + XP * h]
    out["along"] = np.repeat(along, FRAMES, axis=0).astype(np.float32)
    out["mask"] = np.repeat(mask, FRAMES, axis=0).astype(np.float32)
    out["t3"] = fine_table(t3)
    out["t18"] = fine_table(t3.T)

    ang = w * (np.outer(px, full) % N)
    c, s = np.cos(ang), np.sin(ang)
    for h in range(2):
        t5 = np.zeros((256, 256))
        lanes = slice(64 * h, 64 * h + NX)
        lanes2 = slice(128 + 64 * h, 128 + 64 * h + NX)
        t5[lanes, :N], t5[lanes2, :N] = c, s
        t5[lanes, 128 : 128 + N], t5[lanes2, 128 : 128 + N] = -s, c
        out[f"t5{h}"] = right_table(t5)
        t16 = np.zeros((256, 256))
        t16[:N, lanes], t16[128 : 128 + N, lanes] = c.T, -s.T
        t16[:N, lanes2], t16[128 : 128 + N, lanes2] = s.T, c.T
        out[f"t16{h}"] = right_table(t16)
    l7 = np.zeros((176, 96))
    l7[:N, :NX], l7[:N, 48 : 48 + NX] = c.T, s.T
    l7[N:, :NX], l7[N:, 48 : 48 + NX] = -s.T, c.T
    out["l7"] = left_table(l7 * root)
    l15 = np.zeros((96, 176))
    l15[:NX, :N], l15[:NX, N:] = c, -s
    l15[48 : 48 + NX, :N], l15[48 : 48 + NX, N:] = s, c
    out["l15"] = left_table(l15)

    ang = w * (np.outer(full, full) % N)
    c, s = np.cos(ang), np.sin(ang)
    t9 = np.zeros((128, 256))
    t9[:N, :N], t9[:N, 128 : 128 + N] = c, -s
    out["t9"] = right_table(t9)
    l10 = np.zeros((96, 176))
    l10[:NU, :N], l10[:NU, N:] = c[:NU], s[:NU]
    l10[48 : 48 + NU, :N], l10[48 : 48 + NU, N:] = -s[:NU], c[:NU]
    out["l10"] = left_table(l10)
    t12 = np.zeros((256, 256))
    t12[:N, :N], t12[128 : 128 + N, :N] = c, -s
    t12[:N, 128 : 128 + N], t12[128 : 128 + N, 128 : 128 + N] = s, c
    out["t12"] = right_table(t12)
    weight = np.full((NU,), 2.0)
    weight[0] = weight[44] = 1.0
    weight = weight * (-2.0) * 2.0 * root
    l13 = np.zeros((96, 96))
    l13[:N, :NU], l13[:N, 48 : 48 + NU] = c[:, :NU] * weight, -s[:, :NU] * weight
    out["l13"] = left_table(l13)

    profile = 0.5 - 0.5 * np.cos(2.0 * np.pi * (full + 0.5) / N)
    window = np.zeros((N, 128), np.float32)
    window[:, :N] = profile[:, None] * profile[None, :]
    out["window"] = window
    signed = (full + 44) % N - 44.0
    freq = np.zeros((2, 48, 128), np.float32)
    freq[0, :NU, :] = signed[:NU, None]
    freq[1, :, :N] = signed[None, :]
    out["freq"] = (freq * (-w)).astype(np.float32)

    flip = np.zeros((128, 128), ml_dtypes.bfloat16)
    for v in range(N):
        flip[(N - v) % N, v] = 1
    out["flip"] = np.concatenate([flip, flip], axis=0)
    place = np.zeros((176, 192), ml_dtypes.bfloat16)
    for u in range(N):
        if u < NU:
            place[u, u] = 1
            place[N + u, 48 + u] = 1
        else:
            place[u, 96 + N - u] = 1
            place[N + u, 144 + N - u] = -1
    out["place"] = np.concatenate([place, place], axis=1)
    return out


def fine_table(table):
    hi = table.astype(np.float32).astype(ml_dtypes.bfloat16)
    rest = table - hi.astype(np.float64)
    mid = rest.astype(np.float32).astype(ml_dtypes.bfloat16)
    low = (rest - mid.astype(np.float64)).astype(np.float32).astype(ml_dtypes.bfloat16)
    return np.concatenate([hi, hi, mid, mid, low, hi], axis=0)


def split(x):
    hi = x.astype(bf16)
    return hi, (x - hi.astype(f32)).astype(bf16)


def dot(a, b):
    return jnp.dot(a, b, preferred_element_type=f32)


def right(x, table):
    hi, lo = split(x)
    return dot(jnp.concatenate([hi, lo, hi], axis=1), table)


def fine(x, table):
    hi = x.astype(bf16)
    rest = x - hi.astype(f32)
    mid = rest.astype(bf16)
    low = (rest - mid.astype(f32)).astype(bf16)
    return dot(jnp.concatenate([hi, mid, hi, mid, hi, low], axis=1), table)


def left(table, x):
    hi, lo = split(x)
    return dot(table, jnp.concatenate([hi, lo, hi], axis=0))


def sincos(x):
    k = jnp.floor(x * (2.0 / math.pi) + 0.5)
    r = x - k * 1.5703125
    r = r - k * 4.8351287841796875e-4
    r = r - k * 3.1385570764541626e-07
    z = r * r
    s = r + r * z * (-1.6666654611e-1 + z * (8.3321608736e-3 + z * -1.9515295891e-4))
    c = 1.0 - 0.5 * z + z * z * (
        4.166664568298827e-2 + z * (-1.388731625493765e-3 + z * 2.443315711809948e-5)
    )
    q = k.astype(jnp.int32)
    swap = (q & 1) == 1
    sin = jnp.where(swap, c, s)
    cos = jnp.where(swap, s, c)
    sin = jnp.where((q & 2) == 2, -sin, sin)
    cos = jnp.where(((q + 1) & 2) == 2, -cos, cos)
    return sin, cos


PACKS = {
    "narrow": ("m1", "m2", "t3", "t18", "flip"),
    "wide": ("t50", "t51", "t160", "t161", "t12", "t9"),
    "left96": ("l7", "l13"),
    "left176": ("l15", "l10"),
    "order": ("place",),
    "real": ("along", "mask", "window", "freq"),
}


@functools.lru_cache
def packed():
    arrays, where = [], {}
    for index, names in enumerate(PACKS.values()):
        rows = []
        for name in names:
            table = tables()[name]
            table = table.reshape(-1, table.shape[-1])
            where[name] = (index, sum(r.shape[0] for r in rows), table.shape[0])
            rows.append(table)
        arrays.append(np.concatenate(rows, axis=0))
    return arrays, where


def kernel(*refs):
    where = packed()[1]
    count = len(PACKS)
    frames, shifts_in, coefs_in, anchors_in, assign_in = refs[:5]
    packs_in = refs[5 : 5 + count]
    obj, out = refs[5 + count : 7 + count]
    packs = refs[7 + count : 7 + 2 * count]
    (
        shifts,
        coefs,
        anchors,
        assign,
        slots,
        strip,
        send,
        recv,
        csend,
        crecv,
        nsend,
        nrecv,
        esend,
        ramp,
        curs,
        pup,
        foc,
        tra,
        dat,
        ysc,
        asc,
        gsc,
        hsc,
        small_sem,
        pack_sem,
        load_sem,
        halo_send,
        halo_recv,
        msg_send,
        msg_recv,
        c_send,
        c_recv,
        n_send,
        n_recv,
        e_send,
        e_recv,
        e_own,
    ) = refs[7 + 2 * count :]

    def tab(name):
        index, start, rows = where[name]
        return packs[index][start : start + rows, :]

    me_frm, me_pat = lax.axis_index("frm"), lax.axis_index("pat")
    half, side = lax.div(me_pat, 2), lax.rem(me_pat, 2)
    loop = lax.fori_loop

    small = [
        pltpu.make_async_copy(a, b, small_sem.at[i])
        for i, (a, b) in enumerate(
            [(shifts_in, shifts), (coefs_in, coefs), (anchors_in, anchors), (assign_in, assign)]
        )
    ]
    for copy in small:
        copy.start()

    def load(t):
        return pltpu.make_async_copy(
            frames.at[0, :, pl.ds(pl.multiple_of(t * 128, 128), 128)],
            strip.at[t, pl.ds(0, SH), :],
            load_sem.at[t],
        )

    def start_load(t, _):
        load(t).start()
        return 0

    def end_load(t, _):
        load(t).wait()
        return 0

    loop(0, 16, start_load, 0)
    pack_loads = [
        pltpu.make_async_copy(packs_in[i], packs[i], pack_sem.at[i]) for i in range(count)
    ]
    for copy in pack_loads:
        copy.start()

    barrier = pltpu.get_barrier_semaphore()

    def tell(frm, pat):
        pl.semaphore_signal(
            barrier, inc=1, device_id={"frm": frm, "pat": pat}, device_id_type=MESH
        )

    def greet(q, _):
        @pl.when(q != me_frm)
        def _():
            tell(q, me_pat)

        return 0

    loop(0, FRAMES, greet, 0)

    @pl.when(me_pat < GROUPS - 1)
    def _():
        tell(me_frm, me_pat + 1)

    same = half == me_frm

    def greet_late(k, _):
        @pl.when(jnp.logical_not(same & (2 * me_frm + k == me_pat)))
        def _():
            tell(half, 2 * me_frm + k)

        return 0

    loop(0, 2, greet_late, 0)

    @pl.when(me_pat == GROUPS - 1)
    def _():
        strip[:, SH:, :] = jnp.zeros((16, N, 128), f32)

    loop(0, 16, end_load, 0)
    pl.semaphore_wait(
        barrier,
        FRAMES - 1 + (me_pat > 0).astype(jnp.int32) + 2 - same.astype(jnp.int32),
    )

    halo = pltpu.make_async_remote_copy(
        src_ref=strip.at[:, pl.ds(0, N), :],
        dst_ref=strip.at[:, pl.ds(SH, N), :],
        send_sem=halo_send,
        recv_sem=halo_recv,
        device_id={"frm": me_frm, "pat": jnp.maximum(me_pat - 1, 0)},
        device_id_type=MESH,
    )

    @pl.when(me_pat > 0)
    def _():
        halo.start()

    for copy in small:
        copy.wait()

    def order(g, _):
        first = jnp.int32(0)
        second = jnp.int32(0)
        for p in range(PPS - 1, -1, -1):
            hit = assign[p] == g
            second = jnp.where(hit, first, second)
            first = jnp.where(hit, p, first)
        slots[2 * g] = first
        slots[2 * g + 1] = second
        return 0

    loop(0, GROUPS, order, 0)

    def to_peer(source, target, send_sems, recv_sems, q):
        return pltpu.make_async_remote_copy(
            src_ref=source.at[q],
            dst_ref=target.at[me_frm],
            send_sem=send_sems.at[q],
            recv_sem=recv_sems.at[me_frm],
            device_id={"frm": q, "pat": me_pat},
            device_id_type=MESH,
        )

    def from_peer(source, target, send_sems, recv_sems, q):
        return pltpu.make_async_remote_copy(
            src_ref=source.at[q],
            dst_ref=target.at[q],
            send_sem=send_sems.at[q],
            recv_sem=recv_sems.at[q],
            device_id={"frm": q, "pat": me_pat},
            device_id_type=MESH,
        )

    csend[...] = jnp.zeros((FRAMES, 8, 128), f32)

    def send_coefs(i, _):
        q = lax.rem(me_frm + i, FRAMES)
        for j in range(PER):
            csend[q, j : j + 1, :MODES] = coefs[0, pl.ds(slots[PER * q + j], 1), :]
        for k in range(2):
            csend[q, PER + k : PER + k + 1, :] = jnp.zeros((1, 128), f32) + shifts[0, k]

        @pl.when(i > 0)
        def _():
            to_peer(csend, crecv, c_send, c_recv, q).start()

        @pl.when(i == 0)
        def _():
            crecv[me_frm] = csend[me_frm]

        return 0

    loop(0, FRAMES, send_coefs, 0)
    for copy in pack_loads:
        copy.wait()

    def take(source, target, send_sems, recv_sems):
        def one(i, _):
            q = lax.rem(me_frm + i, FRAMES)
            from_peer(source, target, send_sems, recv_sems, q).wait_recv()
            return 0

        loop(1, FRAMES, one, 0)

    def drain(source, target, send_sems, recv_sems):
        def one(i, _):
            q = lax.rem(me_frm + i, FRAMES)
            to_peer(source, target, send_sems, recv_sems, q).wait_send()
            return 0

        loop(1, FRAMES, one, 0)

    take(csend, crecv, c_send, c_recv)
    for j in range(PER):
        curs[j] = jnp.concatenate([crecv[f, j : j + 1, :] for f in range(FRAMES)], axis=0)
    freq = tab("freq")

    def make_ramp(f, _):
        angle = freq[:48] * crecv[f, PER : PER + 1, :] + freq[48:] * crecv[f, PER + 1 : PER + 2, :]
        sin, cos = sincos(angle)
        ramp[f, 0] = cos
        ramp[f, 1] = sin
        return 0

    loop(0, FRAMES, make_ramp, 0)

    def half_spectra(values):
        asc[...] = right(values, tab("t9"))
        for f in range(0, FRAMES, 2):
            stacked = []
            for g in (f, f + 1):
                part = asc[g * N : (g + 1) * N, :]
                stacked.append(jnp.concatenate([part[:, :128], part[:, 128:]], axis=0))
            both = left(tab("l10"), jnp.concatenate(stacked, axis=1))
            yield f, both[:, :128]
            yield f + 1, both[:, 128:]

    def forward(j):
        cab = fine(curs[j], tab("m1"))
        phase = fine(jnp.concatenate([cab] * XP, axis=0) * tab("along"), tab("t3"))
        sin, cos = sincos(phase)
        mask = tab("mask")
        pr, pi = cos * mask, sin * mask
        pup[j, 0] = pr
        pup[j, 1] = pi
        hi, lo = split(jnp.concatenate([pr, pi], axis=1))
        stack = jnp.concatenate([hi, lo, hi], axis=1)
        for h in range(2):
            both = dot(stack, tab(f"t5{h}"))
            ysc[h] = both[:, :128]
            ysc[2 + h] = both[:, 128:]
        spreads = []
        for f in range(0, FRAMES, 2):
            pair = []
            for g in (f, f + 1):
                pair.append(
                    jnp.concatenate([ysc[h, pl.ds(g, XP, FRAMES), :] for h in range(4)], axis=0)
                )
            both = left(tab("l7"), jnp.concatenate(pair, axis=1))
            for g in (0, 1):
                one = both[:, 128 * g : 128 * g + 128]
                foc[j, f + g] = one
                spreads.append(one[:N] * one[:N] + one[N:] * one[N:])
        for f, one in half_spectra(jnp.concatenate(spreads, axis=0)):
            tra[j, f] = one

    def backward(j, step):
        cre = jnp.zeros((48, 128), f32)
        cim = jnp.zeros((48, 128), f32)
        den = jnp.full((48, 128), DAMPING, f32)
        for f in range(FRAMES):
            tre, tim = tra[j, f, :48], tra[j, f, 48:]
            dre, dim = dat[f, :48], dat[f, 48:]
            cre = cre + (dre * tre + dim * tim)
            cim = cim + (dim * tre - dre * tim)
            den = den + (tre * tre + tim * tim)
        ere, eim = cre / den, cim / den
        esend[j, 0, :48] = ere
        esend[j, 1, :48] = eim
        for f in range(FRAMES):
            tre, tim = tra[j, f, :48], tra[j, f, 48:]
            mre = dat[f, :48] - (ere * tre - eim * tim)
            mim = dat[f, 48:] - (ere * tim + eim * tre)
            gsc[f * 48 : f * 48 + 48, :128] = ere * mre + eim * mim
            gsc[f * 48 : f * 48 + 48, 128:] = ere * mim - eim * mre
        gsc[...] = right(gsc[...], tab("t12"))
        for f in range(0, FRAMES, 2):
            pair = []
            for g in (f, f + 1):
                part = gsc[g * 48 : g * 48 + 48, :]
                pair.append(jnp.concatenate([part[:, :128], part[:, 128:]], axis=0))
            grad = left(tab("l13"), jnp.concatenate(pair, axis=1))[:N]
            pair = []
            for g in (0, 1):
                one = grad[:, 128 * g : 128 * g + 128]
                pair.append(
                    jnp.concatenate([one * foc[j, f + g, :N], one * foc[j, f + g, N:]], axis=0)
                )
            both = left(tab("l15"), jnp.concatenate(pair, axis=1))
            for g in (0, 1):
                re, im = (both[k : k + 48, 128 * g : 128 * g + 128] for k in (0, 48))
                for h in range(2):
                    rows = slice(XP * h, XP * h + XP)
                    hsc[2 * h, pl.ds(f + g, XP, FRAMES), :] = re[rows]
                    hsc[2 * h + 1, pl.ds(f + g, XP, FRAMES), :] = im[rows]
        back = None
        for h in range(2):
            one = right(jnp.concatenate([hsc[2 * h], hsc[2 * h + 1]], axis=1), tab(f"t16{h}"))
            back = one if back is None else back + one
        grad = back[:, 128:] * pup[j, 0] - back[:, :128] * pup[j, 1]
        gab = fine(grad, tab("t18")) * tab("along")
        acc = gab[:FRAMES]
        for i in range(1, XP):
            acc = acc + gab[i * FRAMES : (i + 1) * FRAMES]
        curs[j] = curs[j] - step * fine(acc, tab("m2"))

    def first_half(j, _):
        forward(j)
        return 0

    loop(0, EARLY, first_half, 0)

    @pl.when(me_pat < GROUPS - 1)
    def _():
        halo.wait_recv()

    lane = lax.broadcasted_iota(jnp.int32, (N, 128), 1)
    top = me_pat * SH

    def pixels(j, q):
        return pltpu.make_async_remote_copy(
            src_ref=send.at[j, q],
            dst_ref=recv.at[j, me_frm],
            send_sem=msg_send.at[j, q],
            recv_sem=msg_recv.at[j, me_frm],
            device_id={"frm": q, "pat": me_pat},
            device_id_type=MESH,
        )

    def pixels_from(j, q):
        return pltpu.make_async_remote_copy(
            src_ref=send.at[j, q],
            dst_ref=recv.at[j, q],
            send_sem=msg_send.at[j, q],
            recv_sem=msg_recv.at[j, q],
            device_id={"frm": q, "pat": me_pat},
            device_id_type=MESH,
        )

    def cut(n, _):
        j, q = lax.div(n, FRAMES), lax.rem(me_frm + 1 + lax.rem(n, FRAMES), FRAMES)
        p = slots[PER * q + j]
        row = jnp.clip(anchors[0, p] - top, 0, SH - 1)
        col = anchors[1, p]
        tile = jnp.clip(lax.shift_right_logical(col, 7), 0, 15)
        off = col & 127
        a = strip[tile, pl.ds(row, N), :]
        b = strip[jnp.minimum(tile + 1, 15), pl.ds(row, N), :]
        turn = (128 - off) & 127
        patch = jnp.where(lane < 128 - off, pltpu.roll(a, turn, 1), pltpu.roll(b, turn, 1))

        @pl.when(q != me_frm)
        def _():
            send[j, q] = patch
            pixels(j, q).start()

        @pl.when(q == me_frm)
        def _():
            recv[j, me_frm] = patch

        return 0

    loop(0, PER * FRAMES, cut, 0)
    loop(EARLY, PER, first_half, 0)

    def estimate(j):
        return pltpu.make_async_remote_copy(
            src_ref=esend.at[j],
            dst_ref=obj.at[2 * side + lax.rem(j, 2)],
            send_sem=e_send.at[j],
            recv_sem=e_recv.at[2 * side + lax.rem(j, 2)],
            device_id={"frm": half, "pat": 2 * me_frm + lax.div(j, 2)},
            device_id_type=MESH,
        )

    def estimate_here(j):
        return pltpu.make_async_copy(
            esend.at[j], obj.at[2 * side + lax.rem(j, 2)], e_own.at[j]
        )

    def estimate_stays(j):
        return same & (2 * me_frm + lax.div(j, 2) == me_pat)

    def work(j, _):
        def arrived(i, _):
            pixels_from(j, lax.rem(me_frm + i, FRAMES)).wait_recv()
            return 0

        loop(1, FRAMES, arrived, 0)
        window = tab("window")
        parts = []
        total = jnp.zeros((N, 128), f32)
        for f in range(FRAMES):
            part = jnp.where(lane < N, recv[j, f], 0.0) * window
            total = total + part * part
            parts.append(part)
        energy = jnp.sum(total) * float(N * N)
        for f, one in half_spectra(jnp.concatenate(parts, axis=0)):
            re, im = one[:48], one[48:]
            cos, sin = ramp[f, 0], ramp[f, 1]
            dat[f, :48] = re * cos - im * sin
            dat[f, 48:] = re * sin + im * cos
        step = (STEP * FRAMES) / (jnp.zeros((FRAMES, 128), f32) + energy)

        def iterate(t, _):
            backward(j, step)

            @pl.when(t < ITERS - 1)
            def _():
                forward(j)

            return 0

        loop(0, ITERS, iterate, 0)
        spectrum = jnp.concatenate([esend[j, 0, :48], esend[j, 1, :48]], axis=0) * (1.0 / N)
        hi, lo = split(spectrum)
        flipped = dot(jnp.concatenate([hi, lo], axis=1), tab("flip"))
        hi, lo = split(jnp.concatenate([spectrum, flipped], axis=0))
        whole = dot(tab("place"), jnp.concatenate([hi, lo], axis=0))
        esend[j, 0] = whole[:N]
        esend[j, 1] = whole[N:]

        @pl.when(jnp.logical_not(estimate_stays(j)))
        def _():
            estimate(j).start()

        @pl.when(estimate_stays(j))
        def _():
            estimate_here(j).start()

        for f in range(FRAMES):
            nsend[f, pl.ds(j, 1), :] = curs[j, f : f + 1, :]
        return 0

    nsend[...] = jnp.zeros((FRAMES, 8, 128), f32)
    loop(0, PER, work, 0)

    def give(i, _):
        q = lax.rem(me_frm + i, FRAMES)
        to_peer(nsend, nrecv, n_send, n_recv, q).start()
        return 0

    loop(1, FRAMES, give, 0)
    nrecv[me_frm] = nsend[me_frm]

    def end_estimate(j, _):
        stays = estimate_stays(j)

        @pl.when(jnp.logical_not(stays))
        def _():
            estimate(j).wait_send()

        @pl.when(stays)
        def _():
            estimate_here(j).wait()

        return 0

    def end_pixels(n, _):
        j, q = lax.div(n, FRAMES), lax.rem(n, FRAMES)

        @pl.when(q != me_frm)
        def _():
            pixels(j, q).wait_send()

        return 0

    loop(0, PER * FRAMES, end_pixels, 0)
    drain(csend, crecv, c_send, c_recv)

    @pl.when(me_pat > 0)
    def _():
        halo.wait_send()

    take(nsend, nrecv, n_send, n_recv)

    out[...] = jnp.zeros((PPS, 128), f32)
    lane1 = lax.broadcasted_iota(jnp.int32, (PPS, 1), 0)

    def place_back(n, _):
        row = nrecv[lax.div(n, PER), pl.ds(lax.rem(n, PER), 1), :]
        out[...] = jnp.where(lane1 == slots[n], row, out[...])
        return 0

    loop(0, PPS, place_back, 0)
    loop(0, PER, end_estimate, 0)
    drain(nsend, nrecv, n_send, n_recv)

    def estimate_from(k, _):
        source = 2 * me_frm + lax.div(k, 2)

        @pl.when(jnp.logical_not(same & (source == me_pat)))
        def _():
            pltpu.make_async_remote_copy(
                src_ref=esend.at[k],
                dst_ref=obj.at[k],
                send_sem=e_send.at[k],
                recv_sem=e_recv.at[k],
                device_id={"frm": half, "pat": source},
                device_id_type=MESH,
            ).wait_recv()

        return 0

    loop(0, 4, estimate_from, 0)


EARLY = 3


def shards(frames, shifts, coefficients, anchors, assign):
    arrays = packed()[0]
    hbm = pl.BlockSpec(memory_space=pltpu.HBM)
    sems = pltpu.SemaphoreType.DMA
    obj, new = pl.pallas_call(
        kernel,
        in_specs=[hbm] * (5 + len(arrays)),
        out_specs=[hbm, pl.BlockSpec(memory_space=pltpu.VMEM)],
        out_shape=[
            jax.ShapeDtypeStruct((PER, 2, N, 128), f32),
            jax.ShapeDtypeStruct((PPS, 128), f32),
        ],
        scratch_shapes=[pltpu.VMEM(a.shape, a.dtype) for a in arrays]
        + [
            pltpu.SMEM((1, 2), f32),
            pltpu.VMEM((1, PPS, MODES), f32),
            pltpu.SMEM((2, PPS), jnp.int32),
            pltpu.SMEM((PPS,), jnp.int32),
            pltpu.SMEM((PPS,), jnp.int32),
            pltpu.VMEM((16, SH + N, 128), f32),
            pltpu.VMEM((PER, FRAMES, N, 128), f32),
            pltpu.VMEM((PER, FRAMES, N, 128), f32),
            pltpu.VMEM((FRAMES, 8, 128), f32),
            pltpu.VMEM((FRAMES, 8, 128), f32),
            pltpu.VMEM((FRAMES, 8, 128), f32),
            pltpu.VMEM((FRAMES, 8, 128), f32),
            pltpu.VMEM((PER, 2, N, 128), f32),
            pltpu.VMEM((FRAMES, 2, 48, 128), f32),
            pltpu.VMEM((PER, FRAMES, 128), f32),
            pltpu.VMEM((PER, 2, XP * FRAMES, 128), f32),
            pltpu.VMEM((PER, FRAMES, 176, 128), f32),
            pltpu.VMEM((PER, FRAMES, 96, 128), f32),
            pltpu.VMEM((FRAMES, 96, 128), f32),
            pltpu.VMEM((4, XP * FRAMES, 128), f32),
            pltpu.VMEM((FRAMES * N, 256), f32),
            pltpu.VMEM((FRAMES * 48, 256), f32),
            pltpu.VMEM((4, XP * FRAMES, 128), f32),
            sems((4,)),
            sems((len(arrays),)),
            sems((16,)),
            sems,
            sems,
            sems((PER, FRAMES)),
            sems((PER, FRAMES)),
            sems((FRAMES,)),
            sems((FRAMES,)),
            sems((FRAMES,)),
            sems((FRAMES,)),
            sems((PER,)),
            sems((PER,)),
            sems((PER,)),
        ],
        compiler_params=pltpu.CompilerParams(
            collective_id=0, has_side_effects=True, vmem_limit_bytes=56 << 20
        ),
        name="deconvolve",
    )(frames, shifts, coefficients, anchors.T, assign, *[jnp.asarray(a) for a in arrays])
    return new[None, :, :MODES], obj[:, :, :, :N].reshape(PER, 2, N * N)


def solution(mesh):
    in_specs = (
        P("frm", "pat", None),
        P("frm", None),
        P("frm", "pat", None),
        P("pat", None),
        P("pat"),
    )
    out_specs = (P("frm", "pat", None), P(("pat", "frm"), None, None))
    return jax.shard_map(shards, mesh=mesh, in_specs=in_specs, out_specs=out_specs, check_vma=False)
```

time: 381 us -> 74.7 us (0.20); the launches traced: 374 us -> 74.5 us
  matrix products: 145 us -> 0 us
  local copies, waits for them, and re-layouts: 118 us -> 3.37 us
  Pallas kernels: 0 us -> 70.5 us
  other arithmetic: 51.6 us -> 0 us
  starting transfers between devices: 39.7 us -> 0 us
  waiting for transfers between devices: 15.7 us -> 0 us
    dot_general x66 -> x0, matrix products: 145 us -> none  [the longest x32 67.1 us: apply_columns(): return jnp.einsum('vk,ukb->uvb', table, values, precision=highest)]
    gather x98 -> x0, local copies, waits for them, and re-layouts: 87.3 us -> none
    pallas_call x0 -> x1, Pallas kernels: none -> 70.5 us  [shards(): pl.pallas_call(kernel, in_specs=[hbm] * (5 + len(arrays)), out_specs=[hbm...]
    all_to_all x6 -> x0, starting transfers between devices: 37.1 us -> none  [the longest x1 12.1 us: shards(): lax.all_to_all(finals, 'pat', split_axis=1, concat_axis=1, tiled=True)]
    mul x9 -> x0, other arithmetic: 34.6 us -> none  [the longest x5 28.6 us: zernike_table(): surfaces.append(surface * inside)]
    all_to_all x6 -> x0, waiting for transfers between devices: 15.7 us -> none  [the longest x1 4.62 us: shards(): lax.all_to_all(finals, 'pat', split_axis=1, concat_axis=1, tiled=True)]
    another operation x3 -> x0, local copies, waits for them, and re-layouts: 14.2 us -> none  [the longest x2 11.9 us: zernike_table(): return (jnp.stack(surfaces), inside)]
    reduce_sum x8 -> x0, other arithmetic: 11.1 us -> none  [the longest x6 10.2 us: frame_total(): jnp.sum(values.reshape(PATCH, PATCH, frames_here, patches_here), axis=2)]
  transfers between devices with their start and end apart: 7 -> 0, of which waited for: 4 -> 0; matrix products, arithmetic and copies ran while one was open for 23% -> 0% of each run, Pallas kernels for 0% -> 0%
where the time goes in v2:
time: 74.7 us; the launch traced here: 74.5 us
  Pallas kernels  70.5 us (94%)
  local copies, waits for them, and re-layouts  3.37 us (5%)
    pallas_call x1, Pallas kernels, shards(): pl.pallas_call(kernel, in_specs=[hbm] * (5 + len(arrays)), out_specs=[hbm...  70.5 us
    reshape x1, local copies, waits for them, and re-layouts, shards(): return (new[None, :, :MODES], obj[:, :, :, :N].reshape(PER, 2, N * N))  2.05 us

profile of v2, /device:TPU:7, one launch (start us, length us, event | category | flops | bytes accessed | tf_op | source)
XLA Modules:
  0.0 74.5 jit_solution(6683253498034864820)
XLA Ops:
  0.6 70.5 %deconvolve.1 = (f32[4,2,88,128]{3,2,1,0:T(8,128)}, f32[32,128]{1,0:T(8,128)}) custom-call(f32[1,128,2048]{2,1,0:T(8,128)} %refs_0_.1, f32[1,2]{1,0:T(1,128)} %refs_1_.1, f32[1,32,40]{2,1,0:T(8,128)} %refs_2_.1, s32[2,32]{1,0:T(2,128)} %bitcast.7, s32[32]{0:T(128)} %refs_4_.1, bf16[3328,128]{1,0:T(8,128)(2,1)} %constant.12.clone.refs_5_, ...), custom_call_target="tpu_custom_call" | custom-call | tf_op jit(solution)/shard_map/deconvolve/pallas_call | solution.py:819
  71.1 1.3 %slice_bitcast_fusion = f32[1,32,40]{2,1,0:T(8,128)} fusion(f32[32,128]{1,0:T(8,128)} %get-tuple-element.4), kind=kLoop, calls=%fused_computation | loop fusion | bytes 10240 | tf_op jit(solution)/shard_map/broadcast_in_dim | solution.py:872
  72.5 2.0 %reshape.7 = f32[4,2,7744]{2,1,0:T(2,128)} reshape(f32[4,2,88,88]{3,2,1,0:T(8,128)} %bitcast.6) | data formatting | bytes 495616 | tf_op jit(solution)/shard_map/reshape | solution.py:872

commit v3 on v2

--- a/solution.py
+++ b/solution.py
@@ -406,29 +406,6 @@
 
     loop(0, 2, greet_late, 0)
 
-    @pl.when(me_pat == GROUPS - 1)
-    def _():
-        strip[:, SH:, :] = jnp.zeros((16, N, 128), f32)
-
-    loop(0, 16, end_load, 0)
-    pl.semaphore_wait(
-        barrier,
-        FRAMES - 1 + (me_pat > 0).astype(jnp.int32) + 2 - same.astype(jnp.int32),
-    )
-
-    halo = pltpu.make_async_remote_copy(
-        src_ref=strip.at[:, pl.ds(0, N), :],
-        dst_ref=strip.at[:, pl.ds(SH, N), :],
-        send_sem=halo_send,
-        recv_sem=halo_recv,
-        device_id={"frm": me_frm, "pat": jnp.maximum(me_pat - 1, 0)},
-        device_id_type=MESH,
-    )
-
-    @pl.when(me_pat > 0)
-    def _():
-        halo.start()
-
     for copy in small:
         copy.wait()
 
@@ -467,24 +444,45 @@
 
     csend[...] = jnp.zeros((FRAMES, 8, 128), f32)
 
-    def send_coefs(i, _):
-        q = lax.rem(me_frm + i, FRAMES)
+    def fill_coefs(q, _):
         for j in range(PER):
             csend[q, j : j + 1, :MODES] = coefs[0, pl.ds(slots[PER * q + j], 1), :]
         for k in range(2):
             csend[q, PER + k : PER + k + 1, :] = jnp.zeros((1, 128), f32) + shifts[0, k]
-
-        @pl.when(i > 0)
-        def _():
-            to_peer(csend, crecv, c_send, c_recv, q).start()
-
-        @pl.when(i == 0)
-        def _():
-            crecv[me_frm] = csend[me_frm]
-
-        return 0
-
-    loop(0, FRAMES, send_coefs, 0)
+        return 0
+
+    loop(0, FRAMES, fill_coefs, 0)
+    crecv[me_frm] = csend[me_frm]
+
+    @pl.when(me_pat == GROUPS - 1)
+    def _():
+        strip[:, SH:, :] = jnp.zeros((16, N, 128), f32)
+
+    loop(0, 16, end_load, 0)
+    pl.semaphore_wait(
+        barrier,
+        FRAMES - 1 + (me_pat > 0).astype(jnp.int32) + 2 - same.astype(jnp.int32),
+    )
+
+    def send_coefs(i, _):
+        to_peer(csend, crecv, c_send, c_recv, lax.rem(me_frm + i, FRAMES)).start()
+        return 0
+
+    loop(1, FRAMES, send_coefs, 0)
+
+    halo = pltpu.make_async_remote_copy(
+        src_ref=strip.at[:, pl.ds(0, N), :],
+        dst_ref=strip.at[:, pl.ds(SH, N), :],
+        send_sem=halo_send,
+        recv_sem=halo_recv,
+        device_id={"frm": me_frm, "pat": jnp.maximum(me_pat - 1, 0)},
+        device_id_type=MESH,
+    )
+
+    @pl.when(me_pat > 0)
+    def _():
+        halo.start()
+
     for copy in pack_loads:
         copy.wait()
 
@@ -558,7 +556,42 @@
         for f, one in half_spectra(jnp.concatenate(spreads, axis=0)):
             tra[j, f] = one
 
-    def backward(j, step):
+    def estimate(j):
+        return pltpu.make_async_remote_copy(
+            src_ref=esend.at[j],
+            dst_ref=obj.at[2 * side + lax.rem(j, 2)],
+            send_sem=e_send.at[j],
+            recv_sem=e_recv.at[2 * side + lax.rem(j, 2)],
+            device_id={"frm": half, "pat": 2 * me_frm + lax.div(j, 2)},
+            device_id_type=MESH,
+        )
+
+    def estimate_here(j):
+        return pltpu.make_async_copy(
+            esend.at[j], obj.at[2 * side + lax.rem(j, 2)], e_own.at[j]
+        )
+
+    def estimate_stays(j):
+        return same & (2 * me_frm + lax.div(j, 2) == me_pat)
+
+    def send_estimate(j, ere, eim):
+        spectrum = jnp.concatenate([ere, eim], axis=0) * (1.0 / N)
+        hi, lo = split(spectrum)
+        flipped = dot(jnp.concatenate([hi, lo], axis=1), tab("flip"))
+        hi, lo = split(jnp.concatenate([spectrum, flipped], axis=0))
+        whole = dot(tab("place"), jnp.concatenate([hi, lo], axis=0))
+        esend[j, 0] = whole[:N]
+        esend[j, 1] = whole[N:]
+
+        @pl.when(jnp.logical_not(estimate_stays(j)))
+        def _():
+            estimate(j).start()
+
+        @pl.when(estimate_stays(j))
+        def _():
+            estimate_here(j).start()
+
+    def backward(j, step, last):
         cre = jnp.zeros((48, 128), f32)
         cim = jnp.zeros((48, 128), f32)
         den = jnp.full((48, 128), DAMPING, f32)
@@ -569,8 +602,8 @@
             cim = cim + (dim * tre - dre * tim)
             den = den + (tre * tre + tim * tim)
         ere, eim = cre / den, cim / den
-        esend[j, 0, :48] = ere
-        esend[j, 1, :48] = eim
+        if last:
+            send_estimate(j, ere, eim)
         for f in range(FRAMES):
             tre, tim = tra[j, f, :48], tra[j, f, 48:]
             mre = dat[f, :48] - (ere * tre - eim * tim)
@@ -667,24 +700,6 @@
     loop(0, PER * FRAMES, cut, 0)
     loop(EARLY, PER, first_half, 0)
 
-    def estimate(j):
-        return pltpu.make_async_remote_copy(
-            src_ref=esend.at[j],
-            dst_ref=obj.at[2 * side + lax.rem(j, 2)],
-            send_sem=e_send.at[j],
-            recv_sem=e_recv.at[2 * side + lax.rem(j, 2)],
-            device_id={"frm": half, "pat": 2 * me_frm + lax.div(j, 2)},
-            device_id_type=MESH,
-        )
-
-    def estimate_here(j):
-        return pltpu.make_async_copy(
-            esend.at[j], obj.at[2 * side + lax.rem(j, 2)], e_own.at[j]
-        )
-
-    def estimate_stays(j):
-        return same & (2 * me_frm + lax.div(j, 2) == me_pat)
-
     def work(j, _):
         def arrived(i, _):
             pixels_from(j, lax.rem(me_frm + i, FRAMES)).wait_recv()
@@ -706,32 +721,10 @@
             dat[f, 48:] = re * sin + im * cos
         step = (STEP * FRAMES) / (jnp.zeros((FRAMES, 128), f32) + energy)
 
-        def iterate(t, _):
-            backward(j, step)
-
-            @pl.when(t < ITERS - 1)
-            def _():
+        for t in range(ITERS):
+            if t > 0:
                 forward(j)
-
-            return 0
-
-        loop(0, ITERS, iterate, 0)
-        spectrum = jnp.concatenate([esend[j, 0, :48], esend[j, 1, :48]], axis=0) * (1.0 / N)
-        hi, lo = split(spectrum)
-        flipped = dot(jnp.concatenate([hi, lo], axis=1), tab("flip"))
-        hi, lo = split(jnp.concatenate([spectrum, flipped], axis=0))
-        whole = dot(tab("place"), jnp.concatenate([hi, lo], axis=0))
-        esend[j, 0] = whole[:N]
-        esend[j, 1] = whole[N:]
-
-        @pl.when(jnp.logical_not(estimate_stays(j)))
-        def _():
-            estimate(j).start()
-
-        @pl.when(estimate_stays(j))
-        def _():
-            estimate_here(j).start()
-
+            backward(j, step, t == ITERS - 1)
         for f in range(FRAMES):
             nsend[f, pl.ds(j, 1), :] = curs[j, f : f + 1, :]
         return 0

time: 74.7 us -> 69.2 us (0.926)
  the two profiles are of different devices: /device:TPU:7 before, /device:TPU:2 now
where the time goes in v3:
time: 69.2 us; the launch traced here: 69 us
  Pallas kernels  65 us (94%)
  local copies, waits for them, and re-layouts  3.37 us (5%)
    pallas_call x1, Pallas kernels, shards(): pl.pallas_call(kernel, in_specs=[hbm] * (5 + len(arrays)), out_specs=[hbm...  65 us
    reshape x1, local copies, waits for them, and re-layouts, shards(): return (new[None, :, :MODES], obj[:, :, :, :N].reshape(PER, 2, N * N))  2.05 us

profile of v3, /device:TPU:2, one launch (start us, length us, event | category | flops | bytes accessed | tf_op | source)
XLA Modules:
  0.0 69.0 jit_solution(1400780625180556285)
XLA Ops:
  0.6 65.0 %deconvolve.1 = (f32[4,2,88,128]{3,2,1,0:T(8,128)}, f32[32,128]{1,0:T(8,128)}) custom-call(f32[1,128,2048]{2,1,0:T(8,128)} %refs_0_.1, f32[1,2]{1,0:T(1,128)} %refs_1_.1, f32[1,32,40]{2,1,0:T(8,128)} %refs_2_.1, s32[2,32]{1,0:T(2,128)} %bitcast.7, s32[32]{0:T(128)} %refs_4_.1, bf16[3328,128]{1,0:T(8,128)(2,1)} %constant.12.clone.refs_5_, ...), custom_call_target="tpu_custom_call" | custom-call | tf_op jit(solution)/shard_map/deconvolve/pallas_call | solution.py:812
  65.6 1.3 %slice_bitcast_fusion = f32[1,32,40]{2,1,0:T(8,128)} fusion(f32[32,128]{1,0:T(8,128)} %get-tuple-element.4), kind=kLoop, calls=%fused_computation | loop fusion | bytes 10240 | tf_op jit(solution)/shard_map/broadcast_in_dim | solution.py:865
  66.9 2.0 %reshape.7 = f32[4,2,7744]{2,1,0:T(2,128)} reshape(f32[4,2,88,88]{3,2,1,0:T(8,128)} %bitcast.6) | data formatting | bytes 495616 | tf_op jit(solution)/shard_map/reshape | solution.py:865

commit v4 on v3

--- a/solution.py
+++ b/solution.py
@@ -14,6 +14,8 @@
 MODES = 40
 ITERS = 2
 FRAMES = 8
+ITEMS = 16
+TEAMS = 2
 SH = 128
 PPS = 32
 GROUPS = 16
@@ -138,24 +140,24 @@
         for i in range(XP):
             if i + XP * h < NX:
                 mask[i, 64 * h : 64 * h + NX] = aperture[i + XP * h]
-    out["along"] = np.repeat(along, FRAMES, axis=0).astype(np.float32)
-    out["mask"] = np.repeat(mask, FRAMES, axis=0).astype(np.float32)
+    out["along"] = np.repeat(along, ITEMS, axis=0).astype(np.float32)
+    out["mask"] = np.repeat(mask, ITEMS, axis=0).astype(np.float32)
     out["t3"] = fine_table(t3)
     out["t18"] = fine_table(t3.T)
 
     ang = w * (np.outer(px, full) % N)
     c, s = np.cos(ang), np.sin(ang)
-    for h in range(2):
-        t5 = np.zeros((256, 256))
-        lanes = slice(64 * h, 64 * h + NX)
-        lanes2 = slice(128 + 64 * h, 128 + 64 * h + NX)
-        t5[lanes, :N], t5[lanes2, :N] = c, s
-        t5[lanes, 128 : 128 + N], t5[lanes2, 128 : 128 + N] = -s, c
-        out[f"t5{h}"] = right_table(t5)
-        t16 = np.zeros((256, 256))
-        t16[:N, lanes], t16[128 : 128 + N, lanes] = c.T, -s.T
-        t16[:N, lanes2], t16[128 : 128 + N, lanes2] = s.T, c.T
-        out[f"t16{h}"] = right_table(t16)
+    t5p = np.zeros((128, 256))
+    t5p[:NX, :N], t5p[64 : 64 + NX, :N] = c, s
+    t5p[:NX, 128 : 128 + N], t5p[64 : 64 + NX, 128 : 128 + N] = -s, c
+    out["t5p"] = right_table(t5p)
+    t16p = np.zeros((256, 128))
+    t16p[:N, :NX], t16p[128 : 128 + N, :NX] = c.T, -s.T
+    t16p[:N, 64 : 64 + NX], t16p[128 : 128 + N, 64 : 64 + NX] = s.T, c.T
+    hi, lo = halves(t16p)
+    out["t16p"] = np.concatenate(
+        [np.concatenate([hi, lo], axis=1), np.concatenate([hi, 0 * hi], axis=1)], axis=0
+    )
     l7 = np.zeros((176, 96))
     l7[:N, :NX], l7[:N, 48 : 48 + NX] = c.T, s.T
     l7[N:, :NX], l7[N:, 48 : 48 + NX] = -s.T, c.T
@@ -238,12 +240,24 @@
     rest = x - hi.astype(f32)
     mid = rest.astype(bf16)
     low = (rest - mid.astype(f32)).astype(bf16)
-    return dot(jnp.concatenate([hi, mid, hi, mid, hi, low], axis=1), table)
+    k = x.shape[1]
+    t2 = jnp.concatenate([table[:k], table[2 * k : 3 * k]], axis=1)
+    tl = table[4 * k : 5 * k]
+    two = dot(jnp.concatenate([hi, mid], axis=1), jnp.concatenate([t2, t2], axis=0))
+    rest = dot(jnp.concatenate([hi, low], axis=1), jnp.concatenate([tl, table[:k]], axis=0))
+    return two[:, :128] + (two[:, 128:] + rest)
 
 
 def left(table, x):
     hi, lo = split(x)
-    return dot(table, jnp.concatenate([hi, lo, hi], axis=0))
+    k, m = x.shape[0], table.shape[0]
+    if k > 128:
+        t2 = jnp.concatenate([table[:, :k], table[:, 2 * k:]], axis=0)
+        a = dot(t2, hi)
+        return a[:m] + (a[m:] + dot(table[:, :k], lo))
+    rest = jnp.concatenate([table[:, 2 * k:], jnp.zeros((m, k), bf16)], axis=1)
+    a = dot(jnp.concatenate([table[:, :2 * k], rest], axis=0), jnp.concatenate([hi, lo], axis=0))
+    return a[:m] + a[m:]
 
 
 def sincos(x):
@@ -267,7 +281,7 @@
 
 PACKS = {
     "narrow": ("m1", "m2", "t3", "t18", "flip"),
-    "wide": ("t50", "t51", "t160", "t161", "t12", "t9"),
+    "wide": ("t5p", "t16p", "t12", "t9"),
     "left96": ("l7", "l13"),
     "left176": ("l15", "l10"),
     "order": ("place",),
@@ -503,8 +517,11 @@
         loop(1, FRAMES, one, 0)
 
     take(csend, crecv, c_send, c_recv)
-    for j in range(PER):
-        curs[j] = jnp.concatenate([crecv[f, j : j + 1, :] for f in range(FRAMES)], axis=0)
+    for b in range(TEAMS):
+        curs[b] = jnp.concatenate(
+            [crecv[f, 2 * b + i : 2 * b + i + 1, :] for i in range(2) for f in range(FRAMES)],
+            axis=0,
+        )
     freq = tab("freq")
 
     def make_ramp(f, _):
@@ -518,7 +535,7 @@
 
     def half_spectra(values):
         asc[...] = right(values, tab("t9"))
-        for f in range(0, FRAMES, 2):
+        for f in range(0, ITEMS, 2):
             stacked = []
             for g in (f, f + 1):
                 part = asc[g * N : (g + 1) * N, :]
@@ -527,34 +544,38 @@
             yield f, both[:, :128]
             yield f + 1, both[:, 128:]
 
-    def forward(j):
-        cab = fine(curs[j], tab("m1"))
+    low_lanes = lax.broadcasted_iota(jnp.int32, (XP * ITEMS, 128), 1) < 64
+
+    def forward(b):
+        cab = fine(curs[b], tab("m1"))
         phase = fine(jnp.concatenate([cab] * XP, axis=0) * tab("along"), tab("t3"))
         sin, cos = sincos(phase)
         mask = tab("mask")
         pr, pi = cos * mask, sin * mask
-        pup[j, 0] = pr
-        pup[j, 1] = pi
-        hi, lo = split(jnp.concatenate([pr, pi], axis=1))
-        stack = jnp.concatenate([hi, lo, hi], axis=1)
+        pup[b, 0] = pr
+        pup[b, 1] = pi
         for h in range(2):
-            both = dot(stack, tab(f"t5{h}"))
+            if h == 0:
+                mix = jnp.where(low_lanes, pr, pltpu.roll(pi, 64, 1))
+            else:
+                mix = jnp.where(low_lanes, pltpu.roll(pr, 64, 1), pi)
+            both = right(mix, tab("t5p"))
             ysc[h] = both[:, :128]
             ysc[2 + h] = both[:, 128:]
         spreads = []
-        for f in range(0, FRAMES, 2):
+        for f in range(0, ITEMS, 2):
             pair = []
             for g in (f, f + 1):
                 pair.append(
-                    jnp.concatenate([ysc[h, pl.ds(g, XP, FRAMES), :] for h in range(4)], axis=0)
+                    jnp.concatenate([ysc[h, pl.ds(g, XP, ITEMS), :] for h in range(4)], axis=0)
                 )
             both = left(tab("l7"), jnp.concatenate(pair, axis=1))
             for g in (0, 1):
                 one = both[:, 128 * g : 128 * g + 128]
-                foc[j, f + g] = one
+                foc[b, f + g] = one
                 spreads.append(one[:N] * one[:N] + one[N:] * one[N:])
         for f, one in half_spectra(jnp.concatenate(spreads, axis=0)):
-            tra[j, f] = one
+            tra[b, f] = one
 
     def estimate(j):
         return pltpu.make_async_remote_copy(
@@ -574,7 +595,7 @@
     def estimate_stays(j):
         return same & (2 * me_frm + lax.div(j, 2) == me_pat)
 
-    def send_estimate(j, ere, eim):
+    def fill_estimate(j, ere, eim):
         spectrum = jnp.concatenate([ere, eim], axis=0) * (1.0 / N)
         hi, lo = split(spectrum)
         flipped = dot(jnp.concatenate([hi, lo], axis=1), tab("flip"))
@@ -583,6 +604,7 @@
         esend[j, 0] = whole[:N]
         esend[j, 1] = whole[N:]
 
+    def send_estimate(j):
         @pl.when(jnp.logical_not(estimate_stays(j)))
         def _():
             estimate(j).start()
@@ -591,27 +613,31 @@
         def _():
             estimate_here(j).start()
 
-    def backward(j, step, last):
-        cre = jnp.zeros((48, 128), f32)
-        cim = jnp.zeros((48, 128), f32)
-        den = jnp.full((48, 128), DAMPING, f32)
-        for f in range(FRAMES):
-            tre, tim = tra[j, f, :48], tra[j, f, 48:]
-            dre, dim = dat[f, :48], dat[f, 48:]
-            cre = cre + (dre * tre + dim * tim)
-            cim = cim + (dim * tre - dre * tim)
-            den = den + (tre * tre + tim * tim)
-        ere, eim = cre / den, cim / den
+    def backward(b, step, last):
+        for i in range(2):
+            cre = jnp.zeros((48, 128), f32)
+            cim = jnp.zeros((48, 128), f32)
+            den = jnp.full((48, 128), DAMPING, f32)
+            for f in range(FRAMES * i, FRAMES * (i + 1)):
+                tre, tim = tra[b, f, :48], tra[b, f, 48:]
+                dre, dim = dat[f, :48], dat[f, 48:]
+                cre = cre + (dre * tre + dim * tim)
+                cim = cim + (dim * tre - dre * tim)
+                den = den + (tre * tre + tim * tim)
+            ere, eim = cre / den, cim / den
+            for f in range(FRAMES * i, FRAMES * (i + 1)):
+                tre, tim = tra[b, f, :48], tra[b, f, 48:]
+                mre = dat[f, :48] - (ere * tre - eim * tim)
+                mim = dat[f, 48:] - (ere * tim + eim * tre)
+                gsc[f * 48 : f * 48 + 48, :128] = ere * mre + eim * mim
+                gsc[f * 48 : f * 48 + 48, 128:] = ere * mim - eim * mre
+            if last:
+                fill_estimate(2 * b + i, ere, eim)
         if last:
-            send_estimate(j, ere, eim)
-        for f in range(FRAMES):
-            tre, tim = tra[j, f, :48], tra[j, f, 48:]
-            mre = dat[f, :48] - (ere * tre - eim * tim)
-            mim = dat[f, 48:] - (ere * tim + eim * tre)
-            gsc[f * 48 : f * 48 + 48, :128] = ere * mre + eim * mim
-            gsc[f * 48 : f * 48 + 48, 128:] = ere * mim - eim * mre
+            send_estimate(2 * b)
+            send_estimate(2 * b + 1)
         gsc[...] = right(gsc[...], tab("t12"))
-        for f in range(0, FRAMES, 2):
+        for f in range(0, ITEMS, 2):
             pair = []
             for g in (f, f + 1):
                 part = gsc[g * 48 : g * 48 + 48, :]
@@ -621,25 +647,28 @@
             for g in (0, 1):
                 one = grad[:, 128 * g : 128 * g + 128]
                 pair.append(
-                    jnp.concatenate([one * foc[j, f + g, :N], one * foc[j, f + g, N:]], axis=0)
+                    jnp.concatenate([one * foc[b, f + g, :N], one * foc[b, f + g, N:]], axis=0)
                 )
             both = left(tab("l15"), jnp.concatenate(pair, axis=1))
             for g in (0, 1):
                 re, im = (both[k : k + 48, 128 * g : 128 * g + 128] for k in (0, 48))
                 for h in range(2):
                     rows = slice(XP * h, XP * h + XP)
-                    hsc[2 * h, pl.ds(f + g, XP, FRAMES), :] = re[rows]
-                    hsc[2 * h + 1, pl.ds(f + g, XP, FRAMES), :] = im[rows]
-        back = None
+                    hsc[2 * h, pl.ds(f + g, XP, ITEMS), :] = re[rows]
+                    hsc[2 * h + 1, pl.ds(f + g, XP, ITEMS), :] = im[rows]
+        sides = []
         for h in range(2):
-            one = right(jnp.concatenate([hsc[2 * h], hsc[2 * h + 1]], axis=1), tab(f"t16{h}"))
-            back = one if back is None else back + one
-        grad = back[:, 128:] * pup[j, 0] - back[:, :128] * pup[j, 1]
+            hi, lo = split(jnp.concatenate([hsc[2 * h], hsc[2 * h + 1]], axis=1))
+            one = dot(jnp.concatenate([hi, lo], axis=1), tab("t16p"))
+            sides.append(one[:, :128] + one[:, 128:])
+        gre = jnp.where(low_lanes, sides[0], pltpu.roll(sides[1], 64, 1))
+        gim = jnp.where(low_lanes, pltpu.roll(sides[0], 64, 1), sides[1])
+        grad = gim * pup[b, 0] - gre * pup[b, 1]
         gab = fine(grad, tab("t18")) * tab("along")
-        acc = gab[:FRAMES]
+        acc = gab[:ITEMS]
         for i in range(1, XP):
-            acc = acc + gab[i * FRAMES : (i + 1) * FRAMES]
-        curs[j] = curs[j] - step * fine(acc, tab("m2"))
+            acc = acc + gab[i * ITEMS : (i + 1) * ITEMS]
+        curs[b] = curs[b] - step * fine(acc, tab("m2"))
 
     def first_half(j, _):
         forward(j)
@@ -698,39 +727,43 @@
         return 0
 
     loop(0, PER * FRAMES, cut, 0)
-    loop(EARLY, PER, first_half, 0)
-
-    def work(j, _):
+    loop(EARLY, TEAMS, first_half, 0)
+
+    def work(b, _):
         def arrived(i, _):
-            pixels_from(j, lax.rem(me_frm + i, FRAMES)).wait_recv()
+            for k in range(2):
+                pixels_from(2 * b + k, lax.rem(me_frm + i, FRAMES)).wait_recv()
             return 0
 
         loop(1, FRAMES, arrived, 0)
         window = tab("window")
-        parts = []
-        total = jnp.zeros((N, 128), f32)
-        for f in range(FRAMES):
-            part = jnp.where(lane < N, recv[j, f], 0.0) * window
-            total = total + part * part
-            parts.append(part)
-        energy = jnp.sum(total) * float(N * N)
+        parts, steps = [], []
+        for i in range(2):
+            total = jnp.zeros((N, 128), f32)
+            for f in range(FRAMES):
+                part = jnp.where(lane < N, recv[2 * b + i, f], 0.0) * window
+                total = total + part * part
+                parts.append(part)
+            energy = jnp.sum(total) * float(N * N)
+            steps.append((STEP * FRAMES) / (jnp.zeros((FRAMES, 128), f32) + energy))
         for f, one in half_spectra(jnp.concatenate(parts, axis=0)):
             re, im = one[:48], one[48:]
-            cos, sin = ramp[f, 0], ramp[f, 1]
+            cos, sin = ramp[f % FRAMES, 0], ramp[f % FRAMES, 1]
             dat[f, :48] = re * cos - im * sin
             dat[f, 48:] = re * sin + im * cos
-        step = (STEP * FRAMES) / (jnp.zeros((FRAMES, 128), f32) + energy)
-
+        step = jnp.concatenate(steps, axis=0)
         for t in range(ITERS):
             if t > 0:
-                forward(j)
-            backward(j, step, t == ITERS - 1)
-        for f in range(FRAMES):
-            nsend[f, pl.ds(j, 1), :] = curs[j, f : f + 1, :]
+                forward(b)
+            backward(b, step, t == ITERS - 1)
+        for i in range(2):
+            for f in range(FRAMES):
+                row = FRAMES * i + f
+                nsend[f, pl.ds(2 * b + i, 1), :] = curs[b, row : row + 1, :]
         return 0
 
     nsend[...] = jnp.zeros((FRAMES, 8, 128), f32)
-    loop(0, PER, work, 0)
+    loop(0, TEAMS, work, 0)
 
     def give(i, _):
         q = lax.rem(me_frm + i, FRAMES)
@@ -802,7 +835,7 @@
     loop(0, 4, estimate_from, 0)
 
 
-EARLY = 3
+EARLY = 0
 
 
 def shards(frames, shifts, coefficients, anchors, assign):
@@ -833,15 +866,15 @@
             pltpu.VMEM((FRAMES, 8, 128), f32),
             pltpu.VMEM((PER, 2, N, 128), f32),
             pltpu.VMEM((FRAMES, 2, 48, 128), f32),
-            pltpu.VMEM((PER, FRAMES, 128), f32),
-            pltpu.VMEM((PER, 2, XP * FRAMES, 128), f32),
-            pltpu.VMEM((PER, FRAMES, 176, 128), f32),
-            pltpu.VMEM((PER, FRAMES, 96, 128), f32),
-            pltpu.VMEM((FRAMES, 96, 128), f32),
-            pltpu.VMEM((4, XP * FRAMES, 128), f32),
-            pltpu.VMEM((FRAMES * N, 256), f32),
-            pltpu.VMEM((FRAMES * 48, 256), f32),
-            pltpu.VMEM((4, XP * FRAMES, 128), f32),
+            pltpu.VMEM((TEAMS, ITEMS, 128), f32),
+            pltpu.VMEM((TEAMS, 2, XP * ITEMS, 128), f32),
+            pltpu.VMEM((TEAMS, ITEMS, 176, 128), f32),
+            pltpu.VMEM((TEAMS, ITEMS, 96, 128), f32),
+            pltpu.VMEM((ITEMS, 96, 128), f32),
+            pltpu.VMEM((4, XP * ITEMS, 128), f32),
+            pltpu.VMEM((ITEMS * N, 256), f32),
+            pltpu.VMEM((ITEMS * 48, 256), f32),
+            pltpu.VMEM((4, XP * ITEMS, 128), f32),
             sems((4,)),
             sems((len(arrays),)),
             sems((16,)),

time: 69.2 us -> 62.4 us (0.902)
  the two profiles are of different devices: /device:TPU:2 before, /device:TPU:7 now
where the time goes in v4:
time: 62.4 us; the launch traced here: 61.5 us
  Pallas kernels  57.5 us (92%)
  local copies, waits for them, and re-layouts  3.37 us (5%)
  between operations  0.64 us (1%)
    pallas_call x1, Pallas kernels, shards(): pl.pallas_call(kernel, in_specs=[hbm] * (5 + len(arrays)), out_specs=[hbm...  57.5 us
    reshape x1, local copies, waits for them, and re-layouts, shards(): return (new[None, :, :MODES], obj[:, :, :, :N].reshape(PER, 2, N * N))  2.05 us
    broadcast_in_dim x1, local copies, waits for them, and re-layouts, shards(): return (new[None, :, :MODES], obj[:, :, :, :N].reshape(PER, 2, N * N))  1.32 us

profile of v4, /device:TPU:7, one launch (start us, length us, event | category | flops | bytes accessed | tf_op | source)
XLA Modules:
  0.0 61.5 jit_solution(10126537440376115380)
XLA Ops:
  0.6 57.5 %deconvolve.1 = (f32[4,2,88,128]{3,2,1,0:T(8,128)}, f32[32,128]{1,0:T(8,128)}) custom-call(f32[1,128,2048]{2,1,0:T(8,128)} %refs_0_.1, f32[1,2]{1,0:T(1,128)} %refs_1_.1, f32[1,32,40]{2,1,0:T(8,128)} %refs_2_.1, s32[2,32]{1,0:T(2,128)} %bitcast.7, s32[32]{0:T(128)} %refs_4_.1, bf16[3328,128]{1,0:T(8,128)(2,1)} %constant.12.clone.refs_5_, ...), custom_call_target="tpu_custom_call" | custom-call | tf_op jit(solution)/shard_map/deconvolve/pallas_call | solution.py:845
  58.2 1.3 %slice_bitcast_fusion = f32[1,32,40]{2,1,0:T(8,128)} fusion(f32[32,128]{1,0:T(8,128)} %get-tuple-element.4), kind=kLoop, calls=%fused_computation | loop fusion | bytes 10240 | tf_op jit(solution)/shard_map/broadcast_in_dim | solution.py:898
  59.5 2.0 %reshape.7 = f32[4,2,7744]{2,1,0:T(2,128)} reshape(f32[4,2,88,88]{3,2,1,0:T(8,128)} %bitcast.6) | data formatting | bytes 495616 | tf_op jit(solution)/shard_map/reshape | solution.py:898

commit v5 on v4

--- a/solution.py
+++ b/solution.py
@@ -24,6 +24,7 @@
 XP = 24
 NU = 45
 PER = 4
+ROWS = 136
 DAMPING = 0.05
 STEP = 64.0
 f32, bf16 = jnp.float32, jnp.bfloat16
@@ -674,8 +675,6 @@
         forward(j)
         return 0
 
-    loop(0, EARLY, first_half, 0)
-
     @pl.when(me_pat < GROUPS - 1)
     def _():
         halo.wait_recv()
@@ -683,29 +682,28 @@
     lane = lax.broadcasted_iota(jnp.int32, (N, 128), 1)
     top = me_pat * SH
 
-    def pixels(j, q):
+    def pixels(b, q):
         return pltpu.make_async_remote_copy(
-            src_ref=send.at[j, q],
-            dst_ref=recv.at[j, me_frm],
-            send_sem=msg_send.at[j, q],
-            recv_sem=msg_recv.at[j, me_frm],
+            src_ref=send.at[b, q],
+            dst_ref=recv.at[b, me_frm],
+            send_sem=msg_send.at[b, q],
+            recv_sem=msg_recv.at[b, me_frm],
             device_id={"frm": q, "pat": me_pat},
             device_id_type=MESH,
         )
 
-    def pixels_from(j, q):
+    def pixels_from(b, q):
         return pltpu.make_async_remote_copy(
-            src_ref=send.at[j, q],
-            dst_ref=recv.at[j, q],
-            send_sem=msg_send.at[j, q],
-            recv_sem=msg_recv.at[j, q],
+            src_ref=send.at[b, q],
+            dst_ref=recv.at[b, q],
+            send_sem=msg_send.at[b, q],
+            recv_sem=msg_recv.at[b, q],
             device_id={"frm": q, "pat": me_pat},
             device_id_type=MESH,
         )
 
-    def cut(n, _):
-        j, q = lax.div(n, FRAMES), lax.rem(me_frm + 1 + lax.rem(n, FRAMES), FRAMES)
-        p = slots[PER * q + j]
+    def patch(slot):
+        p = slots[slot]
         row = jnp.clip(anchors[0, p] - top, 0, SH - 1)
         col = anchors[1, p]
         tile = jnp.clip(lax.shift_right_logical(col, 7), 0, 15)
@@ -713,26 +711,38 @@
         a = strip[tile, pl.ds(row, N), :]
         b = strip[jnp.minimum(tile + 1, 15), pl.ds(row, N), :]
         turn = (128 - off) & 127
-        patch = jnp.where(lane < 128 - off, pltpu.roll(a, turn, 1), pltpu.roll(b, turn, 1))
+        return jnp.where(lane < 128 - off, pltpu.roll(a, turn, 1), pltpu.roll(b, turn, 1))
+
+    def cut(n, _):
+        b, q = lax.div(n, FRAMES), lax.rem(me_frm + 1 + lax.rem(n, FRAMES), FRAMES)
+        one = patch(PER * q + 2 * b)
+        two = pltpu.roll(patch(PER * q + 2 * b + 1), N, 1)
+        upper = jnp.where(lane < N, one, two)
+        lower = jnp.where(
+            lane[:48] < 64,
+            two[:48],
+            pltpu.roll(jnp.concatenate([two[48:], two[80:]], axis=0), 64, 1),
+        )
 
         @pl.when(q != me_frm)
         def _():
-            send[j, q] = patch
-            pixels(j, q).start()
+            send[b, q, :N] = upper
+            send[b, q, N:] = lower
+            pixels(b, q).start()
 
         @pl.when(q == me_frm)
         def _():
-            recv[j, me_frm] = patch
-
-        return 0
-
-    loop(0, PER * FRAMES, cut, 0)
-    loop(EARLY, TEAMS, first_half, 0)
+            recv[b, me_frm, :N] = upper
+            recv[b, me_frm, N:] = lower
+
+        return 0
+
+    loop(0, TEAMS * FRAMES, cut, 0)
+    loop(0, TEAMS, first_half, 0)
 
     def work(b, _):
         def arrived(i, _):
-            for k in range(2):
-                pixels_from(2 * b + k, lax.rem(me_frm + i, FRAMES)).wait_recv()
+            pixels_from(b, lax.rem(me_frm + i, FRAMES)).wait_recv()
             return 0
 
         loop(1, FRAMES, arrived, 0)
@@ -741,7 +751,13 @@
         for i in range(2):
             total = jnp.zeros((N, 128), f32)
             for f in range(FRAMES):
-                part = jnp.where(lane < N, recv[2 * b + i, f], 0.0) * window
+                if i == 0:
+                    part = recv[b, f, :N]
+                else:
+                    rest = recv[b, f, N:]
+                    part = jnp.concatenate([rest, pltpu.roll(rest, 64, 1)[:40]], axis=0)
+                    part = pltpu.roll(jnp.where(lane < N, part, recv[b, f, :N]), 40, 1)
+                part = jnp.where(lane < N, part, 0.0) * window
                 total = total + part * part
                 parts.append(part)
             energy = jnp.sum(total) * float(N * N)
@@ -795,7 +811,7 @@
 
         return 0
 
-    loop(0, PER * FRAMES, end_pixels, 0)
+    loop(0, TEAMS * FRAMES, end_pixels, 0)
     drain(csend, crecv, c_send, c_recv)
 
     @pl.when(me_pat > 0)
@@ -833,9 +849,6 @@
         return 0
 
     loop(0, 4, estimate_from, 0)
-
-
-EARLY = 0
 
 
 def shards(frames, shifts, coefficients, anchors, assign):
@@ -858,8 +871,8 @@
             pltpu.SMEM((PPS,), jnp.int32),
             pltpu.SMEM((PPS,), jnp.int32),
             pltpu.VMEM((16, SH + N, 128), f32),
-            pltpu.VMEM((PER, FRAMES, N, 128), f32),
-            pltpu.VMEM((PER, FRAMES, N, 128), f32),
+            pltpu.VMEM((TEAMS, FRAMES, ROWS, 128), f32),
+            pltpu.VMEM((TEAMS, FRAMES, ROWS, 128), f32),
             pltpu.VMEM((FRAMES, 8, 128), f32),
             pltpu.VMEM((FRAMES, 8, 128), f32),
             pltpu.VMEM((FRAMES, 8, 128), f32),
@@ -880,8 +893,8 @@
             sems((16,)),
             sems,
             sems,
-            sems((PER, FRAMES)),
-            sems((PER, FRAMES)),
+            sems((TEAMS, FRAMES)),
+            sems((TEAMS, FRAMES)),
             sems((FRAMES,)),
             sems((FRAMES,)),
             sems((FRAMES,)),

time: 62.4 us -> 60.9 us (0.976)
  Pallas kernels: 57.5 us -> 56.6 us
    pallas_call x1, Pallas kernels: 57.5 us -> 56.6 us  [shards(): pl.pallas_call(kernel, in_specs=[hbm] * (5 + len(arrays)), out_specs=[hbm...]
where the time goes in v5:
time: 60.9 us; the launch traced here: 60.6 us
  Pallas kernels  56.6 us (93%)
  local copies, waits for them, and re-layouts  3.37 us (6%)
  between operations  0.64 us (1%)
    pallas_call x1, Pallas kernels, shards(): pl.pallas_call(kernel, in_specs=[hbm] * (5 + len(arrays)), out_specs=[hbm...  56.6 us
    reshape x1, local copies, waits for them, and re-layouts, shards(): return (new[None, :, :MODES], obj[:, :, :, :N].reshape(PER, 2, N * N))  2.05 us
    broadcast_in_dim x1, local copies, waits for them, and re-layouts, shards(): return (new[None, :, :MODES], obj[:, :, :, :N].reshape(PER, 2, N * N))  1.32 us

profile of v5, /device:TPU:7, one launch (start us, length us, event | category | flops | bytes accessed | tf_op | source)
XLA Modules:
  0.0 60.6 jit_solution(12449118225943987474)
XLA Ops:
  0.6 56.6 %deconvolve.1 = (f32[4,2,88,128]{3,2,1,0:T(8,128)}, f32[32,128]{1,0:T(8,128)}) custom-call(f32[1,128,2048]{2,1,0:T(8,128)} %refs_0_.1, f32[1,2]{1,0:T(1,128)} %refs_1_.1, f32[1,32,40]{2,1,0:T(8,128)} %refs_2_.1, s32[2,32]{1,0:T(2,128)} %bitcast.7, s32[32]{0:T(128)} %refs_4_.1, bf16[3328,128]{1,0:T(8,128)(2,1)} %constant.12.clone.refs_5_, ...), custom_call_target="tpu_custom_call" | custom-call | tf_op jit(solution)/shard_map/deconvolve/pallas_call | solution.py:858
  57.2 1.3 %slice_bitcast_fusion = f32[1,32,40]{2,1,0:T(8,128)} fusion(f32[32,128]{1,0:T(8,128)} %get-tuple-element.4), kind=kLoop, calls=%fused_computation | loop fusion | bytes 10240 | tf_op jit(solution)/shard_map/broadcast_in_dim | solution.py:911
  58.5 2.0 %reshape.7 = f32[4,2,7744]{2,1,0:T(2,128)} reshape(f32[4,2,88,88]{3,2,1,0:T(8,128)} %bitcast.6) | data formatting | bytes 495616 | tf_op jit(solution)/shard_map/reshape | solution.py:911

commit v6 on v5

--- a/solution.py
+++ b/solution.py
@@ -820,15 +820,12 @@
 
     take(nsend, nrecv, n_send, n_recv)
 
-    out[...] = jnp.zeros((PPS, 128), f32)
-    lane1 = lax.broadcasted_iota(jnp.int32, (PPS, 1), 0)
-
-    def place_back(n, _):
-        row = nrecv[lax.div(n, PER), pl.ds(lax.rem(n, PER), 1), :]
-        out[...] = jnp.where(lane1 == slots[n], row, out[...])
-        return 0
-
-    loop(0, PPS, place_back, 0)
+    index = lax.broadcasted_iota(jnp.int32, (PPS, 128), 0)
+    placed = jnp.zeros((PPS, 128), f32)
+    for n in range(PPS):
+        row = nrecv[n // PER, n % PER : n % PER + 1, :]
+        placed = jnp.where(index == slots[n], row, placed)
+    out[...] = placed
     loop(0, PER, end_estimate, 0)
     drain(nsend, nrecv, n_send, n_recv)
 

time: 60.9 us -> 60.7 us (level)
  no operation moved by 1% of the time
where the time goes in v6:
time: 60.7 us; the launch traced here: 60.4 us
  Pallas kernels  56.4 us (93%)
  local copies, waits for them, and re-layouts  3.37 us (6%)
  between operations  0.64 us (1%)
    pallas_call x1, Pallas kernels, shards(): pl.pallas_call(kernel, in_specs=[hbm] * (5 + len(arrays)), out_specs=[hbm...  56.4 us
    reshape x1, local copies, waits for them, and re-layouts, shards(): return (new[None, :, :MODES], obj[:, :, :, :N].reshape(PER, 2, N * N))  2.05 us
    broadcast_in_dim x1, local copies, waits for them, and re-layouts, shards(): return (new[None, :, :MODES], obj[:, :, :, :N].reshape(PER, 2, N * N))  1.32 us

profile of v6, /device:TPU:7, one launch (start us, length us, event | category | flops | bytes accessed | tf_op | source)
XLA Modules:
  0.0 60.4 jit_solution(147587325342454864)
XLA Ops:
  0.6 56.4 %deconvolve.1 = (f32[4,2,88,128]{3,2,1,0:T(8,128)}, f32[32,128]{1,0:T(8,128)}) custom-call(f32[1,128,2048]{2,1,0:T(8,128)} %refs_0_.1, f32[1,2]{1,0:T(1,128)} %refs_1_.1, f32[1,32,40]{2,1,0:T(8,128)} %refs_2_.1, s32[2,32]{1,0:T(2,128)} %bitcast.7, s32[32]{0:T(128)} %refs_4_.1, bf16[3328,128]{1,0:T(8,128)(2,1)} %constant.12.clone.refs_5_, ...), custom_call_target="tpu_custom_call" | custom-call | tf_op jit(solution)/shard_map/deconvolve/pallas_call | solution.py:855
  57.0 1.3 %slice_bitcast_fusion = f32[1,32,40]{2,1,0:T(8,128)} fusion(f32[32,128]{1,0:T(8,128)} %get-tuple-element.4), kind=kLoop, calls=%fused_computation | loop fusion | bytes 10240 | tf_op jit(solution)/shard_map/broadcast_in_dim | solution.py:908
  58.3 2.0 %reshape.7 = f32[4,2,7744]{2,1,0:T(2,128)} reshape(f32[4,2,88,88]{3,2,1,0:T(8,128)} %bitcast.6) | data formatting | bytes 495616 | tf_op jit(solution)/shard_map/reshape | solution.py:908
